TPU v7x, 128 devices: a whole 4x4x4 slice. The times are simulated.
128 devices in a mesh: owner: 16 (over y, z), suf: 8 (over x, core).
Axes of the slice: x: 4, y: 4, z: 4, core: 2. Of those that a mesh axis runs over, the one named last changes fastest.
Arguments:
- queries: bfloat16 [512, 2, 8192], P('owner', None, 'suf'), may hold values from -40 to 40
- new_keys: bfloat16 [512, 2, 1024], P('owner', None, 'suf'), may hold values from -40 to 40
- new_values: bfloat16 [512, 2, 1024], P('owner', None, 'suf'), may hold values from -6 to 6
- prompt_keys: bfloat16 [16, 8, 8192, 128], P('owner', 'suf'), may hold values from -6 to 6
- prompt_values: bfloat16 [16, 8, 8192, 128], P('owner', 'suf'), may hold values from -6 to 6
- suffix_keys: bfloat16 [512, 256, 1024], P('owner', None, 'suf'), may hold values from -9.5625 to 9.5625
- suffix_values: bfloat16 [512, 256, 1024], P('owner', None, 'suf'), may hold values from -6 to 6
- suffix_len: int32 [512], P('owner'), may hold values from 1 to 256, 65536 in all
- prompt_of_row: int32 [512], P('owner'), may hold values from 0 to 15, as said below
- partner: int32 [512], P('owner'), may hold values from 0 to 511, as said below
- out_weight: bfloat16 [8192, 8192], P(None, 'suf'), may hold values from -0.0625 to 0.0625
Outputs:
- layer_out: bfloat16 [512, 2, 8192], P('owner', None, 'suf')
Inputs may be any that keep to these rules, and one draw needn't show every extreme that they name: `prompt_of_row`: among the 32 rows of one index of owner, no prompt is named by more than 8 rows, and on every index some prompt is named by exactly 8 rows. partner[r] lies among the 32 rows of the same index of owner as r and has the same prompt as r; it may be r itself.
All inputs are finite; a program needn't handle non-finite values. No bound on the sum of `suffix_len` on one device may be relied on, other than what follows from the above.
Results may differ from a plain program's by a relative error of at most 0.005.
Values may be sent and summed in bfloat16 or wider, within the bound.
A program may use at most 128 MiB of HBM per device.

v0:
```python
import jax
import jax.numpy as jnp
from jax import lax
from jax.sharding import PartitionSpec as P

HD = 128
GROUP = 8
CAP = 8


def slot_numbers(prompt_of_row, owners):
    one_hot = (prompt_of_row[:, None] == jnp.arange(owners, dtype=jnp.int32)[None, :]).astype(
        jnp.int32
    )
    within = jnp.sum((jnp.cumsum(one_hot, axis=0) - 1) * one_hot, axis=1)
    return prompt_of_row * CAP + within


def prompt_partial(slot_queries, key_cache, value_cache):
    owners_here = slot_queries.shape[0]
    slot_count = slot_queries.shape[1]
    step_count = slot_queries.shape[2]
    kv_local = key_cache.shape[1]
    length = key_cache.shape[2]
    query_rows = owners_here * slot_count * step_count
    query_block = slot_queries.reshape(query_rows, kv_local, GROUP, HD)
    score_scale = HD ** (-0.5)
    key_span = min(length, 1024)
    block_count = length // key_span
    key_whole = key_cache[0]
    value_whole = value_cache[0]

    def add_block(block_index, state_carry):
        running_max, weight_sum, weighted = state_carry
        key_block = lax.dynamic_slice_in_dim(key_whole, block_index * key_span, key_span, 1)
        value_block = lax.dynamic_slice_in_dim(value_whole, block_index * key_span, key_span, 1)
        scores = (
            jnp.einsum("mkgd,kld->kmgl", query_block, key_block, preferred_element_type=jnp.float32)
            * score_scale
        )
        fresh_max = jnp.maximum(running_max, scores.max(-1))
        decay = jnp.exp(running_max - fresh_max)
        weights = jnp.exp(scores - fresh_max[..., None])
        weight_sum = weight_sum * decay + weights.sum(-1)
        weighted = weighted * decay[..., None] + jnp.einsum(
            "kmgl,kld->kmgd",
            weights.astype(jnp.bfloat16),
            value_block,
            preferred_element_type=jnp.float32,
        )
        return (fresh_max, weight_sum, weighted)

    start_state = (
        jnp.full((kv_local, query_rows, GROUP), -1e30, jnp.float32),
        jnp.zeros((kv_local, query_rows, GROUP), jnp.float32),
        jnp.zeros((kv_local, query_rows, GROUP, HD), jnp.float32),
    )
    running_max, weight_sum, weighted = lax.fori_loop(0, block_count, add_block, start_state)
    normalized = (weighted / weight_sum[..., None]).astype(jnp.bfloat16)
    part_out = jnp.moveaxis(normalized, 0, 1).reshape(
        owners_here, slot_count, step_count, kv_local * GROUP * HD
    )
    part_max = jnp.moveaxis(running_max, 0, 1).reshape(
        owners_here, slot_count, step_count, kv_local * GROUP
    )
    part_sum = jnp.moveaxis(weight_sum, 0, 1).reshape(
        owners_here, slot_count, step_count, kv_local * GROUP
    )
    return (part_out, part_max, part_sum)


def local_partial(query_step, cache_keys, cache_values, lengths, extra_keys, extra_values):
    score_scale = HD ** (-0.5)
    cache_scores = (
        jnp.einsum("rkgd,rskd->rkgs", query_step, cache_keys, preferred_element_type=jnp.float32)
        * score_scale
    )
    valid_mask = (jnp.arange(cache_keys.shape[1], dtype=jnp.int32)[None, :] < lengths[:, None])[
        :, None, None, :
    ]
    cache_scores = jnp.where(valid_mask, cache_scores, -1e30)
    extra_scores = (
        jnp.einsum("rkgd,rekd->rkge", query_step, extra_keys, preferred_element_type=jnp.float32)
        * score_scale
    )
    running_max = jnp.maximum(cache_scores.max(-1), extra_scores.max(-1))
    cache_weights = jnp.where(valid_mask, jnp.exp(cache_scores - running_max[..., None]), 0.0)
    extra_weights = jnp.exp(extra_scores - running_max[..., None])
    weight_sum = cache_weights.sum(-1) + extra_weights.sum(-1)
    weighted = jnp.einsum(
        "rkgs,rskd->rkgd",
        cache_weights.astype(jnp.bfloat16),
        cache_values,
        preferred_element_type=jnp.float32,
    )
    weighted = weighted + jnp.einsum(
        "rkge,rekd->rkgd",
        extra_weights.astype(jnp.bfloat16),
        extra_values,
        preferred_element_type=jnp.float32,
    )
    return (weighted, running_max, weight_sum)


def merge_step(prompt_out, prompt_max, prompt_sum, local_out, local_max, local_sum):
    common_max = jnp.maximum(prompt_max, local_max)
    prompt_scale = prompt_sum * jnp.exp(prompt_max - common_max)
    local_factor = jnp.exp(local_max - common_max)
    combined = (
        prompt_out.astype(jnp.float32) * prompt_scale[..., None]
        + local_out * local_factor[..., None]
    )
    total_sum = prompt_scale + local_sum * local_factor
    return (combined / total_sum[..., None]).astype(jnp.bfloat16)


def body(
    queries,
    new_keys,
    new_values,
    prompt_keys,
    prompt_values,
    suffix_keys,
    suffix_values,
    suffix_len,
    prompt_of_row,
    partner,
    out_weight,
):
    owners = lax.axis_size("owner")
    owner_index = lax.axis_index("owner")
    row_count = queries.shape[0]
    step_count = queries.shape[1]
    width = queries.shape[2]
    kv_local = prompt_keys.shape[1]
    slots = slot_numbers(prompt_of_row, owners)
    every_query, every_prompt = (
        lax.all_gather(queries, "owner", axis=0, tiled=True),
        lax.all_gather(prompt_of_row, "owner", axis=0, tiled=True),
    )
    mine = (every_prompt == owner_index).reshape(owners, row_count).astype(jnp.int32)
    within = jnp.cumsum(mine, axis=1) - 1
    target = jnp.arange(owners, dtype=jnp.int32)[:, None] * CAP + within
    target = jnp.where(mine > 0, target, -1).reshape(-1)
    picker = (jnp.arange(owners * CAP, dtype=jnp.int32)[:, None] == target[None, :]).astype(
        jnp.bfloat16
    )
    packed = jnp.dot(
        picker,
        every_query.reshape(owners * row_count, step_count * width),
        preferred_element_type=jnp.float32,
    )
    packed = packed.astype(jnp.bfloat16).reshape(owners, CAP, step_count, width)
    part_out, part_max, part_sum = prompt_partial(packed, prompt_keys, prompt_values)
    back_out = lax.all_to_all(part_out, "owner", split_axis=0, concat_axis=0, tiled=True)
    back_max, back_sum = (
        lax.all_to_all(part_max, "owner", split_axis=0, concat_axis=0, tiled=True),
        lax.all_to_all(part_sum, "owner", split_axis=0, concat_axis=0, tiled=True),
    )
    row_out = back_out.reshape(owners * CAP, step_count, width)[slots].reshape(
        row_count, step_count, kv_local, GROUP, HD
    )
    row_max = back_max.reshape(owners * CAP, step_count, kv_local * GROUP)[slots].reshape(
        row_count, step_count, kv_local, GROUP
    )
    row_sum = back_sum.reshape(owners * CAP, step_count, kv_local * GROUP)[slots].reshape(
        row_count, step_count, kv_local, GROUP
    )
    query_heads = queries.reshape(row_count, step_count, kv_local, GROUP, HD)
    cache_keys = suffix_keys.reshape(row_count, suffix_keys.shape[1], kv_local, HD)
    cache_values = suffix_values.reshape(row_count, suffix_values.shape[1], kv_local, HD)
    step_keys = new_keys.reshape(row_count, step_count, kv_local, HD)
    step_values = new_values.reshape(row_count, step_count, kv_local, HD)
    parent_local = partner - owner_index * row_count
    first_out, first_max, first_sum = local_partial(
        query_heads[:, 0],
        cache_keys,
        cache_values,
        suffix_len,
        step_keys[:, 0:1],
        step_values[:, 0:1],
    )
    second_keys = jnp.stack([step_keys[parent_local, 0], step_keys[:, 1]], axis=1)
    second_values = jnp.stack([step_values[parent_local, 0], step_values[:, 1]], axis=1)
    second_out, second_max, second_sum = local_partial(
        query_heads[:, 1],
        cache_keys[parent_local],
        cache_values[parent_local],
        suffix_len[parent_local],
        second_keys,
        second_values,
    )
    first_attention = merge_step(
        row_out[:, 0], row_max[:, 0], row_sum[:, 0], first_out, first_max, first_sum
    )
    second_attention = merge_step(
        row_out[:, 1], row_max[:, 1], row_sum[:, 1], second_out, second_max, second_sum
    )
    attention = jnp.stack(
        [first_attention.reshape(row_count, width), second_attention.reshape(row_count, width)],
        axis=1,
    )
    attention = attention.reshape(row_count * step_count, width)
    projected = jnp.dot(
        lax.all_gather(attention, "suf", axis=1, tiled=True),
        out_weight,
        preferred_element_type=jnp.float32,
    )
    return projected.astype(jnp.bfloat16).reshape(row_count, step_count, out_weight.shape[1])


def solution(mesh):
    return jax.shard_map(
        body,
        mesh=mesh,
        in_specs=(
            P("owner", None, "suf"),
            P("owner", None, "suf"),
            P("owner", None, "suf"),
            P("owner", "suf", None, None),
            P("owner", "suf", None, None),
            P("owner", None, "suf"),
            P("owner", None, "suf"),
            P("owner"),
            P("owner"),
            P("owner"),
            P(None, "suf"),
        ),
        out_specs=P("owner", None, "suf"),
        check_vma=False,
    )
```

profile of v0, /device:TPU:1, one launch (start us, length us, event | category | flops | bytes accessed | tf_op | source)
XLA Modules:
  0.0 206.5 jit_solution(3458392514934869294)
XLA Ops:
  6.5 0.7 all-gather.3.cloned.1.call-update
  7.3 1.0 reshape.552
  8.3 1.2 dynamic-slice
  10.2 0.9 dynamic-update-slice
  11.1 14.8 %all-reduce.1 = s32[512]{0:T(512)S(1)} all-reduce(s32[512]{0:T(512)S(1)} %dynamic-update-slice), channel_id=1, replica_groups=mesh['owner'=16,'suf'=8] {'owner'}, use_global_device_ids=true, to_apply=%add.1 | all-reduce | flops 512 | bytes 4096
  28.1 1.4 gather_fusion.5
  29.5 1.4 gather_fusion.7
  31.5 0.7 slice.74
  32.3 0.7 fusion.64
  33.6 1.4 gather_fusion.3
  35.0 2.2 %gather_fusion.4 = bf16[32,256,128]{2,1,0:T(8,128)(2,1)} fusion(bf16[32,256,128]{2,1,0:T(8,128)(2,1)S(1)} %copy-done, s32[1024]{0:T(1024)S(1)} %pad_clamp_fusion), kind=kCustom, calls=%fused_computation.4 | custom fusion | bytes 4194432 | tf_op jit(solution)/shard_map/gather | solution.py:187
  37.5 2.3 %fusion.74 = (f32[32,8]{1,0:T(8,128)S(1)}, f32[32,8,256]{2,1,0:T(8,128)S(1)}) fusion(bf16[32,256,128]{2,1,0:T(8,128)(2,1)} %gather_fusion.4, bf16[32,2,1,8,128]{4,3,1,0,2:T(8,128)(2,1)S(1)} %reshape.552, pred[32,256]{1,0:T(8,128)(4,1)S(1)} %iota_compare_fusion.2), kind=kOutput, calls=%fused_computation.125 | convolution fusion | flops 16973568 | bytes 2434048 | tf_op jit(solution)/shard_map/rkgd,rskd->rkgs/dot_general | solution.py:75
  40.3 0.7 fusion.76
  41.8 0.9 fusion.35
  43.8 0.9 fusion.51
  44.7 12.3 %all-gather.3.cloned.1.call-done = bf16[512,2,1024]{2,1,0:T(2,128)(2,1)} async-done(((bf16[32,2,1024]{2,1,0:T(2,128)(2,1)}), bf16[512,2,1024]{2,1,0:T(2,128)(2,1)}) %all-gather.3.cloned.1.call-update) | async-done | bytes 2097168 | tf_op jit(solution)/shard_map/all_gather | solution.py:138
  57.0 2.2 %copy.51 = bf16[64,8,2,1024]{3,1,2,0:T(8,128)(2,1)S(1)} copy(bf16[64,8,2,1024]{3,2,1,0:T(2,128)(2,1)} %bitcast.162) | data formatting | bytes 4194304
  59.2 1.2 convolution_convert_fusion
  60.5 2.1 %reshape_reshape.3 = bf16[256,1,8,128]{3,2,0,1:T(8,128)(2,1)} reshape(bf16[128,2048]{1,0:T(8,128)(2,1)} %convolution_convert_fusion) | data formatting | bytes 1048576 | tf_op jit(solution)/shard_map/reshape;reshape | solution.py:26
  62.5 1.9 copy.29
  64.4 54.3 %while.18 = (s32[]{:T(128)}, f32[1,256,8]{1,2,0:T(8,128)S(1)}, f32[1,256,8]{1,2,0:T(8,128)S(1)}, f32[1,256,8,128]{3,1,2,0:T(8,128)S(1)}, bf16[1,8192,128]{2,1,0:...) while((s32[]{:T(128)}, f32[1,256,8]{1,2,0:T(8,128)S(1)}, ...), condition=%wide.region_4.5_spmd.clone, body=%wide.region_1.0_spmd.clone.sunk | while | flops 1091317760 | bytes 28442804 | solution.py:58
  64.5 2.4 %bitcast_reduce_fusion.2 = (f32[256,8]{0,1:T(8,128)S(1)}, f32[1024,256,8]{1,0,2:T(8,128)S(1)}) fusion(bf16[256,1,8,128]{3,0,2,1:T(8,128)(2,1)} %get-tuple-element.300, bf16[1,8192,128]{2,1,0:T(8,128)(2,1)} %get-tuple-element.299, s32[]{:T(128)S(6)} %select_n.76), kind=kOutput, calls=%fused_computation.9.clone.1 | convolution fusion | flops 541063168 | bytes 9183236 | tf_op jit(solution)/shard_map/while/body/eval_jaxpr/mkgd,kld->kmgl/dot_general | solution.py:38
  66.9 1.4 fusion.92
  68.2 2.9 %fusion.93 = f32[1,256,8,128]{3,1,2,0:T(8,128)S(1)} fusion(f32[1024,256,8]{1,0,2:T(8,128)S(1)} %get-tuple-element.271, f32[256,8]{0,1:T(8,128)S(1)} %bitcast.161, f32[1,256,8,128]{3,1,2,0:T(8,128)S(1)} %get-tuple-element.287, f32[256,8]{0,1:T(8,128)S(1)} %get-tuple-element.272, pred[]{:T(512)S(6)} %compare.4, ...), kind=kOutput, calls=%fused_computation.17.clone.1 | convolution fusion | flops 543948800 | bytes 10764293 | tf_op jit(solution)/shard_map/while/body/eval_jaxpr/kmgl,kld->kmgd/dot_general | solution.py:45
  71.2 2.4 %bitcast_reduce_fusion.2 = (f32[256,8]{0,1:T(8,128)S(1)}, f32[1024,256,8]{1,0,2:T(8,128)S(1)}) fusion(bf16[256,1,8,128]{3,0,2,1:T(8,128)(2,1)} %get-tuple-element.300, bf16[1,8192,128]{2,1,0:T(8,128)(2,1)} %get-tuple-element.299, s32[]{:T(128)S(6)} %select_n.76), kind=kOutput, calls=%fused_computation.9.clone.1 | convolution fusion | flops 541063168 | bytes 9183236 | tf_op jit(solution)/shard_map/while/body/eval_jaxpr/mkgd,kld->kmgl/dot_general | solution.py:38
  73.6 1.4 fusion.92
  75.0 2.9 %fusion.93 = f32[1,256,8,128]{3,1,2,0:T(8,128)S(1)} fusion(f32[1024,256,8]{1,0,2:T(8,128)S(1)} %get-tuple-element.271, f32[256,8]{0,1:T(8,128)S(1)} %bitcast.161, f32[1,256,8,128]{3,1,2,0:T(8,128)S(1)} %get-tuple-element.287, f32[256,8]{0,1:T(8,128)S(1)} %get-tuple-element.272, pred[]{:T(512)S(6)} %compare.4, ...), kind=kOutput, calls=%fused_computation.17.clone.1 | convolution fusion | flops 543948800 | bytes 10764293 | tf_op jit(solution)/shard_map/while/body/eval_jaxpr/kmgl,kld->kmgd/dot_general | solution.py:45
  78.0 2.4 %bitcast_reduce_fusion.2 = (f32[256,8]{0,1:T(8,128)S(1)}, f32[1024,256,8]{1,0,2:T(8,128)S(1)}) fusion(bf16[256,1,8,128]{3,0,2,1:T(8,128)(2,1)} %get-tuple-element.300, bf16[1,8192,128]{2,1,0:T(8,128)(2,1)} %get-tuple-element.299, s32[]{:T(128)S(6)} %select_n.76), kind=kOutput, calls=%fused_computation.9.clone.1 | convolution fusion | flops 541063168 | bytes 9183236 | tf_op jit(solution)/shard_map/while/body/eval_jaxpr/mkgd,kld->kmgl/dot_general | solution.py:38
  80.4 1.4 fusion.92
  81.8 2.9 %fusion.93 = f32[1,256,8,128]{3,1,2,0:T(8,128)S(1)} fusion(f32[1024,256,8]{1,0,2:T(8,128)S(1)} %get-tuple-element.271, f32[256,8]{0,1:T(8,128)S(1)} %bitcast.161, f32[1,256,8,128]{3,1,2,0:T(8,128)S(1)} %get-tuple-element.287, f32[256,8]{0,1:T(8,128)S(1)} %get-tuple-element.272, pred[]{:T(512)S(6)} %compare.4, ...), kind=kOutput, calls=%fused_computation.17.clone.1 | convolution fusion | flops 543948800 | bytes 10764293 | tf_op jit(solution)/shard_map/while/body/eval_jaxpr/kmgl,kld->kmgd/dot_general | solution.py:45
  84.8 2.4 %bitcast_reduce_fusion.2 = (f32[256,8]{0,1:T(8,128)S(1)}, f32[1024,256,8]{1,0,2:T(8,128)S(1)}) fusion(bf16[256,1,8,128]{3,0,2,1:T(8,128)(2,1)} %get-tuple-element.300, bf16[1,8192,128]{2,1,0:T(8,128)(2,1)} %get-tuple-element.299, s32[]{:T(128)S(6)} %select_n.76), kind=kOutput, calls=%fused_computation.9.clone.1 | convolution fusion | flops 541063168 | bytes 9183236 | tf_op jit(solution)/shard_map/while/body/eval_jaxpr/mkgd,kld->kmgl/dot_general | solution.py:38
  87.2 1.4 fusion.92
  88.6 2.9 %fusion.93 = f32[1,256,8,128]{3,1,2,0:T(8,128)S(1)} fusion(f32[1024,256,8]{1,0,2:T(8,128)S(1)} %get-tuple-element.271, f32[256,8]{0,1:T(8,128)S(1)} %bitcast.161, f32[1,256,8,128]{3,1,2,0:T(8,128)S(1)} %get-tuple-element.287, f32[256,8]{0,1:T(8,128)S(1)} %get-tuple-element.272, pred[]{:T(512)S(6)} %compare.4, ...), kind=kOutput, calls=%fused_computation.17.clone.1 | convolution fusion | flops 543948800 | bytes 10764293 | tf_op jit(solution)/shard_map/while/body/eval_jaxpr/kmgl,kld->kmgd/dot_general | solution.py:45
  91.6 2.4 %bitcast_reduce_fusion.2 = (f32[256,8]{0,1:T(8,128)S(1)}, f32[1024,256,8]{1,0,2:T(8,128)S(1)}) fusion(bf16[256,1,8,128]{3,0,2,1:T(8,128)(2,1)} %get-tuple-element.300, bf16[1,8192,128]{2,1,0:T(8,128)(2,1)} %get-tuple-element.299, s32[]{:T(128)S(6)} %select_n.76), kind=kOutput, calls=%fused_computation.9.clone.1 | convolution fusion | flops 541063168 | bytes 9183236 | tf_op jit(solution)/shard_map/while/body/eval_jaxpr/mkgd,kld->kmgl/dot_general | solution.py:38
  94.0 1.4 fusion.92
  95.4 2.9 %fusion.93 = f32[1,256,8,128]{3,1,2,0:T(8,128)S(1)} fusion(f32[1024,256,8]{1,0,2:T(8,128)S(1)} %get-tuple-element.271, f32[256,8]{0,1:T(8,128)S(1)} %bitcast.161, f32[1,256,8,128]{3,1,2,0:T(8,128)S(1)} %get-tuple-element.287, f32[256,8]{0,1:T(8,128)S(1)} %get-tuple-element.272, pred[]{:T(512)S(6)} %compare.4, ...), kind=kOutput, calls=%fused_computation.17.clone.1 | convolution fusion | flops 543948800 | bytes 10764293 | tf_op jit(solution)/shard_map/while/body/eval_jaxpr/kmgl,kld->kmgd/dot_general | solution.py:45
  98.4 2.4 %bitcast_reduce_fusion.2 = (f32[256,8]{0,1:T(8,128)S(1)}, f32[1024,256,8]{1,0,2:T(8,128)S(1)}) fusion(bf16[256,1,8,128]{3,0,2,1:T(8,128)(2,1)} %get-tuple-element.300, bf16[1,8192,128]{2,1,0:T(8,128)(2,1)} %get-tuple-element.299, s32[]{:T(128)S(6)} %select_n.76), kind=kOutput, calls=%fused_computation.9.clone.1 | convolution fusion | flops 541063168 | bytes 9183236 | tf_op jit(solution)/shard_map/while/body/eval_jaxpr/mkgd,kld->kmgl/dot_general | solution.py:38
  100.8 1.4 fusion.92
  102.2 2.9 %fusion.93 = f32[1,256,8,128]{3,1,2,0:T(8,128)S(1)} fusion(f32[1024,256,8]{1,0,2:T(8,128)S(1)} %get-tuple-element.271, f32[256,8]{0,1:T(8,128)S(1)} %bitcast.161, f32[1,256,8,128]{3,1,2,0:T(8,128)S(1)} %get-tuple-element.287, f32[256,8]{0,1:T(8,128)S(1)} %get-tuple-element.272, pred[]{:T(512)S(6)} %compare.4, ...), kind=kOutput, calls=%fused_computation.17.clone.1 | convolution fusion | flops 543948800 | bytes 10764293 | tf_op jit(solution)/shard_map/while/body/eval_jaxpr/kmgl,kld->kmgd/dot_general | solution.py:45
  105.2 2.4 %bitcast_reduce_fusion.2 = (f32[256,8]{0,1:T(8,128)S(1)}, f32[1024,256,8]{1,0,2:T(8,128)S(1)}) fusion(bf16[256,1,8,128]{3,0,2,1:T(8,128)(2,1)} %get-tuple-element.300, bf16[1,8192,128]{2,1,0:T(8,128)(2,1)} %get-tuple-element.299, s32[]{:T(128)S(6)} %select_n.76), kind=kOutput, calls=%fused_computation.9.clone.1 | convolution fusion | flops 541063168 | bytes 9183236 | tf_op jit(solution)/shard_map/while/body/eval_jaxpr/mkgd,kld->kmgl/dot_general | solution.py:38
  107.6 1.4 fusion.92
  109.0 2.9 %fusion.93 = f32[1,256,8,128]{3,1,2,0:T(8,128)S(1)} fusion(f32[1024,256,8]{1,0,2:T(8,128)S(1)} %get-tuple-element.271, f32[256,8]{0,1:T(8,128)S(1)} %bitcast.161, f32[1,256,8,128]{3,1,2,0:T(8,128)S(1)} %get-tuple-element.287, f32[256,8]{0,1:T(8,128)S(1)} %get-tuple-element.272, pred[]{:T(512)S(6)} %compare.4, ...), kind=kOutput, calls=%fused_computation.17.clone.1 | convolution fusion | flops 543948800 | bytes 10764293 | tf_op jit(solution)/shard_map/while/body/eval_jaxpr/kmgl,kld->kmgd/dot_general | solution.py:45
  112.0 2.4 %bitcast_reduce_fusion.2 = (f32[256,8]{0,1:T(8,128)S(1)}, f32[1024,256,8]{1,0,2:T(8,128)S(1)}) fusion(bf16[256,1,8,128]{3,0,2,1:T(8,128)(2,1)} %get-tuple-element.300, bf16[1,8192,128]{2,1,0:T(8,128)(2,1)} %get-tuple-element.299, s32[]{:T(128)S(6)} %select_n.76), kind=kOutput, calls=%fused_computation.9.clone.1 | convolution fusion | flops 541063168 | bytes 9183236 | tf_op jit(solution)/shard_map/while/body/eval_jaxpr/mkgd,kld->kmgl/dot_general | solution.py:38
  114.4 1.4 fusion.92
  115.7 2.9 %fusion.93 = f32[1,256,8,128]{3,1,2,0:T(8,128)S(1)} fusion(f32[1024,256,8]{1,0,2:T(8,128)S(1)} %get-tuple-element.271, f32[256,8]{0,1:T(8,128)S(1)} %bitcast.161, f32[1,256,8,128]{3,1,2,0:T(8,128)S(1)} %get-tuple-element.287, f32[256,8]{0,1:T(8,128)S(1)} %get-tuple-element.272, pred[]{:T(512)S(6)} %compare.4, ...), kind=kOutput, calls=%fused_computation.17.clone.1 | convolution fusion | flops 543948800 | bytes 10764293 | tf_op jit(solution)/shard_map/while/body/eval_jaxpr/kmgl,kld->kmgd/dot_general | solution.py:45
  118.9 0.8 reshape.556
  119.7 4.7 %all-to-all-start.2 = ((f32[16,1,128]{2,1,0:T(1,128)}), f32[16,1,128]{2,1,0:T(1,128)S(1)}, u32[]{:S(2)}, u32[]{:S(2)}) async-start(f32[16,1,128]{2,1,0:T(1,128)} %reshape.556), calls=%async_computation.2 | async-start | bytes 16384 | tf_op jit(solution)/shard_map/all_to_all | solution.py:157
  124.3 1.4 fusion.49
  125.9 0.8 reshape.554
  126.7 3.9 %all-to-all-done.2 = f32[16,1,128]{2,1,0:T(1,128)S(1)} async-done(((f32[16,1,128]{2,1,0:T(1,128)}), f32[16,1,128]{2,1,0:T(1,128)S(1)}, u32[]{:S(2)}, u32[]{:S(2)}) %all-to-all-start.2) | async-done | bytes 8224 | tf_op jit(solution)/shard_map/all_to_all | solution.py:157
  130.6 3.5 %all-to-all-start.1 = ((f32[16,1,128]{2,1,0:T(1,128)}), f32[16,1,128]{2,1,0:T(1,128)S(1)}, u32[]{:S(2)}, u32[]{:S(2)}) async-start(f32[16,1,128]{2,1,0:T(1,128)} %reshape.554), calls=%async_computation.1 | async-start | bytes 16384 | tf_op jit(solution)/shard_map/all_to_all | solution.py:158
  134.8 0.9 reshape_transpose.9
  135.7 4.7 %all-to-all-done.1 = f32[16,1,128]{2,1,0:T(1,128)S(1)} async-done(((f32[16,1,128]{2,1,0:T(1,128)}), f32[16,1,128]{2,1,0:T(1,128)S(1)}, u32[]{:S(2)}, u32[]{:S(2)}) %all-to-all-start.1) | async-done | bytes 8224 | tf_op jit(solution)/shard_map/all_to_all | solution.py:158
  140.4 3.6 %all-to-all-start = ((bf16[16,8,2,1024]{3,2,1,0:T(2,128)(2,1)}), bf16[16,8,2,1024]{3,2,1,0:T(2,128)(2,1)S(1)}, u32[]{:S(2)}, u32[]{:S(2)}) async-start(bf16[16,8,2,1024]{3,2,1,0:T(2,128)(2,1)} %reshape_transpose.9), calls=%async_computation | async-start | bytes 1048576 | tf_op jit(solution)/shard_map/all_to_all | solution.py:155
  144.3 3.9 %gather_fusion.6 = bf16[32,256,128]{2,1,0:T(8,128)(2,1)} fusion(bf16[32,256,128]{2,1,0:T(8,128)(2,1)} %param.19, s32[1024]{0:T(1024)} %copy-done.31), kind=kCustom, calls=%fused_computation.6 | custom fusion | bytes 4194432 | tf_op jit(solution)/shard_map/gather | solution.py:188
  150.4 1.4 reduce.21
  152.0 0.7 gather_fusion.1
  152.8 1.4 multiply_add_fusion.1
  154.2 1.1 gather_fusion
  155.4 2.1 %fusion.32 = bf16[32,8,128]{2,1,0:T(8,128)(2,1)S(1)} fusion(bf16[32,256,128]{2,1,0:T(8,128)(2,1)} %param.19, f32[32,8,256]{2,1,0:T(8,128)S(1)} %copy-done.3, f32[32,8]{1,0:T(8,128)S(1)} %copy-done.9, pred[32,256]{1,0:T(8,128)(4,1)S(1)} %copy-done.15, bf16[32,2,1,8,128]{4,3,1,0,2:T(8,128)(2,1)S(1)} %reshape.551, f32[32,8]{1,0:T(8,128)} %get-tuple-element.197, ...), kind=kOutput, calls=%fused_computation.48 | convolution fusion | flops 17235968 | bytes 2520064 | tf_op jit(solution)/shard_map/rkgs,rskd->rkgd/dot_general | solution.py:90
  157.6 2.0 fusion.33
  160.7 29.1 %all-gather.5.cloned.1.call-done = bf16[64,8192]{1,0:T(8,128)(2,1)} async-done(((bf16[64,1024]{1,0:T(8,128)(2,1)}), bf16[64,8192]{1,0:T(8,128)(2,1)}) %all-gather.5.cloned.1.call-update) | async-done | bytes 1048592 | tf_op jit(solution)/shard_map/all_gather | solution.py:205
  189.8 9.1 %convolution_convert_fusion.1 = bf16[64,1024]{1,0:T(8,128)(2,1)S(1)} fusion(bf16[64,8192]{1,0:T(8,128)(2,1)} %all-gather.5.cloned.1.call-done, bf16[8192,1024]{1,0:T(8,128)(2,1)} %param.23), kind=kOutput, calls=%fused_computation.39 | convolution fusion | flops 1073807360 | bytes 17956864 | tf_op jit(solution)/shard_map/dot_general | solution.py:204
  199.0 0.7 reshape.446
  (138 shorter events, 11.1 us)
Async XLA Ops:
  6.5 28.5 %copy-start = (bf16[32,256,128]{2,1,0:T(8,128)(2,1)S(1)}, bf16[32,256,128]{2,1,0:T(8,128)(2,1)}, u32[]{:S(2)}) copy-start(bf16[32,256,128]{2,1,0:T(8,128)(2,1)} %param.18) | copy-start | bytes 6291460
  6.5 50.5 %all-gather.3.cloned.1.call-start = ((), (), s32[]{:S(2)}) async-start(), calls=%async_computation.3 | async-start | bytes 2228224 | tf_op jit(solution)/shard_map/all_gather | solution.py:138
  25.8 0.6 copy-start.24
  33.6 3.5 %copy-start.31 = (s32[1024]{0:T(1024)}, s32[1024]{0:T(1024)S(1)}, u32[]{:S(2)}) copy-start(s32[1024]{0:T(1024)S(1)} %pad_clamp_fusion) | copy-start | bytes 12292
  37.2 2.7 %copy-start.19 = (s32[32,16]{1,0:T(8,128)S(1)}, s32[32,16]{1,0:T(8,128)}, u32[]{:S(2)}) copy-start(s32[32,16]{1,0:T(8,128)} %reduce_window_sum.23) | copy-start | bytes 6148
  37.2 2.7 %copy-start.32 = (s32[32]{0:T(128)S(1)}, s32[32]{0:T(128)}, u32[]{:S(2)}) copy-start(s32[32]{0:T(128)} %param.21) | copy-start | bytes 388
  37.2 2.9 %copy-start.1 = (s32[32]{0:T(128)S(1)}, s32[32]{0:T(128)}, u32[]{:S(2)}) copy-start(s32[32]{0:T(128)} %param.20) | copy-start | bytes 388
  37.2 2.9 %copy-start.5 = (bf16[32,2,128]{2,1,0:T(2,128)(2,1)S(1)}, bf16[32,2,128]{2,1,0:T(2,128)(2,1)}, u32[]{:S(2)}) copy-start(bf16[32,2,128]{2,1,0:T(2,128)(2,1)} %param.14) | copy-start | bytes 49156
  37.3 4.4 %copy-start.12 = (pred[32,256]{1,0:T(8,128)(4,1)}, pred[32,256]{1,0:T(8,128)(4,1)S(1)}, u32[]{:S(2)}) copy-start(pred[32,256]{1,0:T(8,128)(4,1)S(1)} %iota_compare_fusion.2) | copy-start | bytes 24580
  37.4 6.3 %copy-start.11 = (f32[32,8,2]{1,2,0:T(2,128)}, f32[32,8,2]{1,2,0:T(2,128)S(1)}, u32[]{:S(2)}) copy-start(f32[32,8,2]{1,2,0:T(2,128)S(1)} %get-tuple-element.217) | copy-start | bytes 6148
  39.8 3.4 %copy-start.25 = (s32[512]{0:T(512)S(1)}, s32[512]{0:T(512)}, u32[]{:S(2)}) copy-start(s32[512]{0:T(512)} %copy-done.24) | copy-start | bytes 6148
  39.8 3.4 %copy-start.29 = (s32[512]{0:T(512)S(1)}, s32[512]{0:T(512)}, u32[]{:S(2)}) copy-start(s32[512]{0:T(512)} %add.123) | copy-start | bytes 6148
  39.8 3.4 %copy-start.4 = (bf16[32,2,128]{2,1,0:T(2,128)(2,1)S(1)}, bf16[32,2,128]{2,1,0:T(2,128)(2,1)}, u32[]{:S(2)}) copy-start(bf16[32,2,128]{2,1,0:T(2,128)(2,1)} %param.15) | copy-start | bytes 49156
  39.8 4.0 %copy-start.20 = (bf16[32,1,1,128]{3,1,0,2:T(2,128)(2,1)S(1)}, bf16[32,1,1,128]{3,1,0,2:T(2,128)(2,1)}, u32[]{:S(2)}) copy-start(bf16[32,1,1,128]{3,1,0,2:T(2,128)(2,1)} %copy.38) | copy-start | bytes 24580
  39.8 3.9 %copy-start.6 = (f32[32,8]{1,0:T(8,128)}, f32[32,8]{1,0:T(8,128)S(1)}, u32[]{:S(2)}) copy-start(f32[32,8]{1,0:T(8,128)S(1)} %max.72) | copy-start | bytes 3076
  40.1 3.7 %copy-start.14 = (pred[32,256]{1,0:T(8,128)(4,1)}, pred[32,256]{1,0:T(8,128)(4,1)S(1)}, u32[]{:S(2)}) copy-start(pred[32,256]{1,0:T(8,128)(4,1)S(1)} %iota_compare_fusion.3) | copy-start | bytes 24580
  40.3 3.5 %copy-start.18 = (f32[32,1,8]{2,1,0:T(1,128)}, f32[32,1,8]{2,1,0:T(1,128)S(1)}, u32[]{:S(2)}) copy-start(f32[32,1,8]{2,1,0:T(1,128)S(1)} %fusion.48) | copy-start | bytes 3076
  41.0 0.7 copy-start.2
  41.7 17.5 %copy-start.8 = (f32[32,8]{1,0:T(8,128)}, f32[32,8]{1,0:T(8,128)S(1)}, u32[]{:S(2)}) copy-start(f32[32,8]{1,0:T(8,128)S(1)} %get-tuple-element.196) | copy-start | bytes 3076
  119.7 10.9 %all-to-all-start.2 = ((f32[16,1,128]{2,1,0:T(1,128)}), f32[16,1,128]{2,1,0:T(1,128)S(1)}, u32[]{:S(2)}, u32[]{:S(2)}) async-start(f32[16,1,128]{2,1,0:T(1,128)} %reshape.556), calls=%async_computation.2 | async-start | bytes 16384 | tf_op jit(solution)/shard_map/all_to_all | solution.py:157
  130.6 9.8 %copy-start.21 = (f32[16,1,128]{2,1,0:T(1,128)}, f32[16,1,128]{2,1,0:T(1,128)S(1)}, u32[]{:S(2)}) copy-start(f32[16,1,128]{2,1,0:T(1,128)S(1)} %all-to-all-done.2) | copy-start | bytes 24580
  130.6 9.8 %all-to-all-start.1 = ((f32[16,1,128]{2,1,0:T(1,128)}), f32[16,1,128]{2,1,0:T(1,128)S(1)}, u32[]{:S(2)}, u32[]{:S(2)}) async-start(f32[16,1,128]{2,1,0:T(1,128)} %reshape.554), calls=%async_computation.1 | async-start | bytes 16384 | tf_op jit(solution)/shard_map/all_to_all | solution.py:158
  134.1 10.2 %copy-start.33 = (s32[32]{0:T(128)S(1)}, s32[32]{0:T(128)}, u32[]{:S(2)}) copy-start(s32[32]{0:T(128)} %compare_select_fusion.1) | copy-start | bytes 388
  140.4 7.8 %copy-start.23 = (f32[16,1,128]{2,1,0:T(1,128)}, f32[16,1,128]{2,1,0:T(1,128)S(1)}, u32[]{:S(2)}) copy-start(f32[16,1,128]{2,1,0:T(1,128)S(1)} %all-to-all-done.1) | copy-start | bytes 24580
  140.4 13.8 %all-to-all-start = ((bf16[16,8,2,1024]{3,2,1,0:T(2,128)(2,1)}), bf16[16,8,2,1024]{3,2,1,0:T(2,128)(2,1)S(1)}, u32[]{:S(2)}, u32[]{:S(2)}) async-start(bf16[16,8,2,1024]{3,2,1,0:T(2,128)(2,1)} %reshape_transpose.9), calls=%async_computation | async-start | bytes 1048576 | tf_op jit(solution)/shard_map/all_to_all | solution.py:155
  144.0 45.8 %all-gather.5.cloned.1.call-start = ((), (), s32[]{:S(2)}) async-start(), calls=%async_computation.4 | async-start | bytes 1179648 | tf_op jit(solution)/shard_map/all_gather | solution.py:205
  144.3 5.5 %copy-start.30 = (s32[1024]{0:T(1024)}, s32[1024]{0:T(1024)S(1)}, u32[]{:S(2)}) copy-start(s32[1024]{0:T(1024)S(1)} %pad_clamp_fusion.1) | copy-start | bytes 12292
  144.3 4.6 %copy-start.22 = (f32[16,1,128]{2,1,0:T(1,128)S(1)}, f32[16,1,128]{2,1,0:T(1,128)}, u32[]{:S(2)}) copy-start(f32[16,1,128]{2,1,0:T(1,128)} %copy-done.21) | copy-start | bytes 24580
  144.3 8.5 %copy-start.7 = (f32[32,8]{1,0:T(8,128)S(1)}, f32[32,8]{1,0:T(8,128)}, u32[]{:S(2)}) copy-start(f32[32,8]{1,0:T(8,128)} %copy-done.6) | copy-start | bytes 3076
  144.3 8.5 %copy-start.9 = (f32[32,8]{1,0:T(8,128)S(1)}, f32[32,8]{1,0:T(8,128)}, u32[]{:S(2)}) copy-start(f32[32,8]{1,0:T(8,128)} %copy-done.8) | copy-start | bytes 3076
  144.3 8.5 %copy-start.16 = (f32[32,8]{1,0:T(8,128)S(1)}, f32[32,8]{1,0:T(8,128)}, u32[]{:S(2)}) copy-start(f32[32,8]{1,0:T(8,128)} %get-tuple-element.220) | copy-start | bytes 3076
  144.3 8.5 %copy-start.17 = (f32[32,8]{1,0:T(8,128)S(1)}, f32[32,8]{1,0:T(8,128)}, u32[]{:S(2)}) copy-start(f32[32,8]{1,0:T(8,128)} %get-tuple-element.221) | copy-start | bytes 3076
  144.3 11.1 %copy-start.3 = (f32[32,8,256]{2,1,0:T(8,128)S(1)}, f32[32,8,256]{2,1,0:T(8,128)}, u32[]{:S(2)}) copy-start(f32[32,8,256]{2,1,0:T(8,128)} %copy-done.2) | copy-start | bytes 786436
  144.3 11.1 %copy-start.15 = (pred[32,256]{1,0:T(8,128)(4,1)S(1)}, pred[32,256]{1,0:T(8,128)(4,1)}, u32[]{:S(2)}) copy-start(pred[32,256]{1,0:T(8,128)(4,1)} %copy-done.14) | copy-start | bytes 24580
  150.3 7.2 %copy-start.10 = (f32[32,8,128]{2,1,0:T(8,128)S(1)}, f32[32,8,128]{2,1,0:T(8,128)}, u32[]{:S(2)}) copy-start(f32[32,8,128]{2,1,0:T(8,128)} %fusion.51) | copy-start | bytes 393220
  150.3 7.2 %copy-start.13 = (pred[32,256]{1,0:T(8,128)(4,1)S(1)}, pred[32,256]{1,0:T(8,128)(4,1)}, u32[]{:S(2)}) copy-start(pred[32,256]{1,0:T(8,128)(4,1)} %copy-done.12) | copy-start | bytes 24580
  154.2 3.4 %copy-start.26 = (f32[32,8]{1,0:T(8,128)S(1)}, f32[32,8]{1,0:T(8,128)}, u32[]{:S(2)}) copy-start(f32[32,8]{1,0:T(8,128)} %get-tuple-element.207) | copy-start | bytes 3076
  154.2 3.4 %copy-start.27 = (f32[32,8]{1,0:T(8,128)S(1)}, f32[32,8]{1,0:T(8,128)}, u32[]{:S(2)}) copy-start(f32[32,8]{1,0:T(8,128)} %get-tuple-element.208) | copy-start | bytes 3076
  155.3 2.3 %copy-start.28 = (f32[32,8]{1,0:T(8,128)S(1)}, f32[32,8]{1,0:T(8,128)}, u32[]{:S(2)}) copy-start(f32[32,8]{1,0:T(8,128)} %get-tuple-element.209) | copy-start | bytes 3076
Sparse Core Ops, SparseCore 0:
  9.5 47.4 all-gather.2
  160.8 28.9 all-gather.4
where the time goes:
time: 208 us; the launch traced here: 207 us
  matrix products  61.4 us (30%)
  waiting for transfers between devices  50.8 us (24%)
  local copies, waits for them, and re-layouts  30.6 us (15%)
  other arithmetic  21.9 us (11%)
  blocking collectives  14.8 us (7%)
  between operations  14.6 us (7%)
  starting transfers between devices  11.9 us (6%)
    all_gather x1, waiting for transfers between devices, body(): lax.all_gather(attention, 'suf', axis=1, tiled=True)  29.1 us
    dot_general x8, matrix products, add_block(): jnp.einsum('kmgl,kld->kmgd', weights.astype(jnp.bfloat16), value_block, p...  23.6 us
    dot_general x8, matrix products, add_block(): jnp.einsum('mkgd,kld->kmgl', query_block, key_block, preferred_element_ty...  19.1 us
    unnamed x1, blocking collectives  14.8 us
    all_gather x1, waiting for transfers between devices, body(): lax.all_gather(queries, 'owner', axis=0, tiled=True)  12.3 us
    reduce_sum x8, other arithmetic, add_block(): weight_sum = weight_sum * decay + weights.sum(-1)  10.9 us
    dot_general x1, matrix products, body(): jnp.dot(lax.all_gather(attention, 'suf', axis=1, tiled=True), out_weight,...  9.12 us
    unnamed x77, local copies, waits for them, and re-layouts  9.08 us
  transfers between devices with their start and end apart: 5, of which 4 were waited for; matrix products, arithmetic and copies ran while one was open for 17% of the time, Pallas kernels for 0%

commit v1 on v0

v1 whole, which is shorter than its diff:
```python
import jax
import jax.numpy as jnp
from jax import lax
from jax.experimental import pallas as pl
from jax.experimental.pallas import tpu as pltpu
from jax.sharding import PartitionSpec as P

MESH = pl.DeviceIdType.MESH
HD = 128
GROUP = 8
CAP = 8
STEPS = 2
SIDE = 4
OWNERS = 16
SUFS = 8
ROWS = 32
SLOT = STEPS * GROUP
BLOCK = CAP * SLOT
LENGTH = 8192
SUFFIX = 256
WIDTH = GROUP * HD
SPAN = 1024
CHUNK = SIDE * BLOCK
SPANS = LENGTH // SPAN
RATE = HD ** (-0.5) * 1.4426950408889634
F32 = jnp.float32
BF16 = jnp.bfloat16


def dot_t(a, b):
    return lax.dot_general(a, b, (((1,), (1,)), ((), ())), preferred_element_type=F32)


def kernel(
    prompt_s, partner_s, length_s,
    q_hbm, nk_hbm, nv_hbm, ks_hbm, vs_hbm, k_hbm, v_hbm, w_hbm,
    out_ref,
    q_v, nk_v, nv_v, ks_v, vs_v, k_v, v_v, vt_v, w_v,
    table_v, table_s, pack_v, rq_v,
    s_v, m_v, l_v, acc_v,
    part_v, stat_v, back_v, bstat_v, bstat_t,
    e_v, pe_v, lo_v, lm_v, ls_v,
    att_v, ag_v, proj_v,
    load_sem, table_sem,
    qsend, qrecv, bsend, brecv, ssend, srecv, gsend, grecv,
):
    me = lax.axis_index("owner")
    lane_f = lax.axis_index("suf")
    y, z = me // SIDE, me % SIDE
    x, core = lane_f // 2, lane_f % 2

    barrier = pltpu.get_barrier_semaphore()
    for d in range(1, OWNERS):
        t = (y + d // SIDE) % SIDE * SIDE + (z + d % SIDE) % SIDE
        pl.semaphore_signal(barrier, inc=1, device_id={"owner": t}, device_id_type=MESH)
    for d in range(1, SUFS):
        t = (lane_f + d) % SUFS
        pl.semaphore_signal(barrier, inc=1, device_id={"suf": t}, device_id_type=MESH)

    pairs = (
        (q_hbm, q_v), (nk_hbm, nk_v), (nv_hbm, nv_v), (ks_hbm, ks_v), (vs_hbm, vs_v),
        (v_hbm, v_v), (k_hbm, k_v), (w_hbm, w_v),
    )
    loads = [
        pltpu.make_async_copy(src, dst, load_sem.at[i]) for i, (src, dst) in enumerate(pairs)
    ]
    for copy in loads:
        copy.start()
    ld_q, ld_nk, ld_nv, ld_ks, ld_vs, ld_v, ld_k, ld_w = loads

    lane = lax.broadcasted_iota(jnp.int32, (8, 128), 1)
    sub = lax.broadcasted_iota(jnp.int32, (8, 128), 0)
    lane_prompt, lane_place = lane // CAP, lane % CAP
    count = jnp.zeros((8, 128), jnp.int32)
    row_of = jnp.zeros((8, 128), jnp.int32)
    own_prompt = jnp.zeros((8, 128), jnp.int32)
    for r in range(ROWS):
        named = prompt_s[r]
        match = lane_prompt == named
        row_of = jnp.where(match & (count == lane_place), r, row_of)
        count = count + jnp.where(match, 1, 0)
        own_prompt = jnp.where(lane == r, named, own_prompt)
    rank = jnp.zeros((8, 128), jnp.int32)
    for r in range(ROWS):
        rank = rank + jnp.where((own_prompt == prompt_s[r]) & (lane > r), 1, 0)
    table_v[...] = jnp.where(sub == 0, row_of, rank % CAP)
    to_smem = pltpu.make_async_copy(table_v, table_s, table_sem)
    to_smem.start()
    to_smem.wait()
    ld_q.wait()

    def pack(i, carry):
        for u in range(8):
            slot = i * 8 + u
            pack_v[pl.ds(pl.multiple_of(slot * SLOT, SLOT), SLOT), :] = q_v[table_s[0, slot]]
        return carry

    lax.fori_loop(0, OWNERS * CAP // 8, pack, 0)

    def block_of(i):
        return pl.ds(pl.multiple_of(i * BLOCK, BLOCK), BLOCK)

    pl.semaphore_wait(barrier, OWNERS - 1 + SUFS - 1)

    def query_copy(t, source):
        return pltpu.make_async_remote_copy(
            src_ref=pack_v.at[block_of(t)], dst_ref=rq_v.at[block_of(source)],
            send_sem=qsend.at[t], recv_sem=qrecv.at[source],
            device_id={"owner": t}, device_id_type=MESH,
        )

    others = []
    for d in range(1, OWNERS):
        others.append((y + d // SIDE) % SIDE * SIDE + (z + d % SIDE) % SIDE)
    for t in others:
        query_copy(t, me).start()
    rq_v[block_of(me), :] = pack_v[block_of(me), :]

    ld_nk.wait()
    ld_nv.wait()
    e_v[...] = dot_t(q_v[...].reshape(ROWS * SLOT, HD), nk_v[...])
    ld_ks.wait()
    ld_vs.wait()
    slot_row = lax.broadcasted_iota(jnp.int32, (SLOT, SUFFIX), 0)
    slot_lane = lax.broadcasted_iota(jnp.int32, (SLOT, SUFFIX), 1)
    extra_row = lax.broadcasted_iota(jnp.int32, (SLOT, 2 * ROWS), 0)
    extra_lane = lax.broadcasted_iota(jnp.int32, (SLOT, 2 * ROWS), 1)

    def local_row(r):
        parent = partner_s[r] % ROWS
        rows = pl.ds(pl.multiple_of(r * SLOT, SLOT), SLOT)
        query = q_v[r]
        first = dot_t(query, ks_v[r])
        second = dot_t(query, ks_v[parent])
        scores = jnp.concatenate([first[:GROUP], second[GROUP:]], axis=0)
        used = jnp.where(slot_row < GROUP, length_s[r], length_s[parent])
        valid = slot_lane < used
        scores = jnp.where(valid, scores, -1e30)
        extra = e_v[rows, :]
        one = jnp.where(extra_row < GROUP, 2 * r, 2 * parent)
        two = jnp.where(extra_row < GROUP, 2 * r, 2 * r + 1)
        extra_valid = (extra_lane == one) | (extra_lane == two)
        extra = jnp.where(extra_valid, extra, -1e30)
        top = jnp.maximum(
            jnp.max(scores, axis=1, keepdims=True), jnp.max(extra, axis=1, keepdims=True)
        )
        weights = jnp.where(valid, jnp.exp2((scores - top) * RATE), 0.0)
        extra = jnp.where(extra_valid, jnp.exp2((extra - top) * RATE), 0.0)
        total = jnp.sum(weights, axis=1, keepdims=True) + jnp.sum(extra, axis=1, keepdims=True)
        weights = weights.astype(BF16)
        first = jnp.dot(weights, vs_v[r], preferred_element_type=F32)
        second = jnp.dot(weights, vs_v[parent], preferred_element_type=F32)
        lo_v[rows, :] = jnp.concatenate([first[:GROUP], second[GROUP:]], axis=0)
        pe_v[rows, :] = extra.astype(BF16)
        lm_v[rows, :] = jnp.broadcast_to(top, (SLOT, HD))
        ls_v[rows, :] = jnp.broadcast_to(total, (SLOT, HD))

    def local_rows(i, carry):
        for u in range(4):
            local_row(i * 4 + u)
        return carry

    lax.fori_loop(0, ROWS // 4, local_rows, 0)
    lo_v[...] += jnp.dot(pe_v[...], nv_v[...], preferred_element_type=F32)

    ld_v.wait()

    def turn(i, carry):
        at = pl.ds(pl.multiple_of(i * 512, 512), 512)
        vt_v[:, at] = v_v[at, :].T
        return carry

    lax.fori_loop(0, LENGTH // 512, turn, 0)
    ld_k.wait()
    for t in others:
        query_copy(t, t).wait_recv()

    def far(c):
        return (y + 1 + c) % SIDE

    def span_of(j):
        return pl.ds(pl.multiple_of(j * SPAN, SPAN), SPAN)

    def score(c, j):
        at = pl.ds(pl.multiple_of(far(c) * CHUNK, CHUNK), CHUNK)
        return dot_t(k_v[span_of(j), :], rq_v[at, :])

    def absorb(place, j):
        s = s_v[place]
        m_old = m_v[...]
        m_new = jnp.maximum(m_old, jnp.max(s, axis=0, keepdims=True))
        p = jnp.exp2((s - m_new[:1]) * RATE)
        decay = jnp.exp2((m_old - m_new) * RATE)
        m_v[...] = m_new
        l_v[...] = l_v[...] * decay + jnp.sum(p.reshape(SPAN // 8, 8, CHUNK), axis=0)
        acc_v[...] = acc_v[...] * decay[:1] + jnp.dot(
            vt_v[:, span_of(j)], p.astype(BF16), preferred_element_type=F32
        )

    def part_copy(t, source):
        return pltpu.make_async_remote_copy(
            src_ref=part_v.at[t], dst_ref=back_v.at[source],
            send_sem=bsend.at[t], recv_sem=brecv.at[source],
            device_id={"owner": t}, device_id_type=MESH,
        )

    def stat_copy(t, source):
        return pltpu.make_async_remote_copy(
            src_ref=stat_v.at[t], dst_ref=bstat_v.at[source],
            send_sem=ssend.at[t], recv_sem=srecv.at[source],
            device_id={"owner": t}, device_id_type=MESH,
        )

    s_v[0] = score(0, 0)

    def chunk(c, carry):
        m_v[...] = jnp.full_like(m_v, -1e30)
        l_v[...] = jnp.zeros_like(l_v)
        acc_v[...] = jnp.zeros_like(acc_v)

        def two_spans(i, inner):
            j = 2 * i
            s_v[1] = score(c, j + 1)
            absorb(0, j)
            last = jnp.where(j + 2 == SPANS, 1, 0)
            s_v[0] = score(c + last, (j + 2) % SPANS)
            absorb(1, j + 1)
            return inner

        lax.fori_loop(0, SPANS // 2, two_spans, 0)
        total = jnp.sum(l_v[...], axis=0, keepdims=True)
        top = m_v[:1, :]
        done = acc_v[...] / total
        for k in range(SIDE):
            t = far(c) * SIDE + k
            cols = slice(k * BLOCK, (k + 1) * BLOCK)
            piece = done[:, cols].T.astype(BF16)
            stats = jnp.concatenate(
                [top[:, cols], total[:, cols], jnp.zeros((6, BLOCK), F32)], axis=0
            )

            @pl.when(t == me)
            def _():
                back_v[t] = piece.reshape(CAP, SLOT, HD)
                bstat_v[t] = stats

            @pl.when(t != me)
            def _():
                part_v[t] = piece.reshape(CAP, SLOT, HD)
                stat_v[t] = stats
                part_copy(t, me).start()
                stat_copy(t, me).start()

        return carry

    lax.fori_loop(0, SIDE, chunk, 0)

    for t in others:
        part_copy(t, t).wait_recv()
        stat_copy(t, t).wait_recv()

    stats = bstat_v[...].reshape(OWNERS * 8, BLOCK)
    bstat_t[...] = stats.T.reshape(CAP, SLOT, OWNERS * 8)
    stat_lane = lax.broadcasted_iota(jnp.int32, (SLOT, OWNERS * 8), 1)

    def merge_row(r):
        named = prompt_s[r]
        rows = pl.ds(pl.multiple_of(r * SLOT, SLOT), SLOT)
        place = table_s[1, r]
        part = back_v[named, place].astype(F32)
        both = bstat_t[place]
        p_max = jnp.sum(jnp.where(stat_lane == named * 8, both, 0.0), axis=1, keepdims=True)
        p_sum = jnp.sum(jnp.where(stat_lane == named * 8 + 1, both, 0.0), axis=1, keepdims=True)
        l_max, l_sum = lm_v[rows, :], ls_v[rows, :]
        top = jnp.maximum(p_max, l_max)
        a = p_sum * jnp.exp2((p_max - top) * RATE)
        b = jnp.exp2((l_max - top) * RATE)
        merged = (a * part + b * lo_v[rows, :]) / (a + b * l_sum)
        for s in range(STEPS):
            at = pl.ds(STEPS * r + s, GROUP, stride=STEPS * ROWS)
            att_v[at, :] = merged[s * GROUP:(s + 1) * GROUP]

    for r in range(ROWS):
        merge_row(r)
    ag_v[lane_f] = att_v[...].astype(BF16)

    def gather_copy(block, to, i):
        return pltpu.make_async_remote_copy(
            src_ref=ag_v.at[block], dst_ref=ag_v.at[block],
            send_sem=gsend.at[i], recv_sem=grecv.at[block],
            device_id={"suf": to}, device_id_type=MESH,
        )

    sibling = x * 2 + 1 - core
    same = [(x + d) % SIDE * 2 + core for d in (1, 3, 2)]
    cross = [(x + d) % SIDE * 2 + 1 - core for d in (1, 3, 2)]
    sent = []
    for i, to in enumerate(same + [sibling]):
        copy = gather_copy(lane_f, to, i)
        copy.start()
        sent.append(copy)

    ld_w.wait()

    def project(block, first=False):
        a = ag_v[block]
        a = jnp.concatenate(
            [a[h * STEPS * ROWS:(h + 1) * STEPS * ROWS] for h in range(GROUP)], axis=1
        )
        w = w_v[pl.ds(pl.multiple_of(block * WIDTH, WIDTH), WIDTH), :]
        term = jnp.dot(a, w, preferred_element_type=F32)
        if first:
            proj_v[...] = term
        else:
            proj_v[...] += term

    def arrive(block):
        gather_copy(block, sibling, 0).wait_recv()

    def forward(i):
        arrive(same[i])
        copy = gather_copy(same[i], sibling, SIDE + i)
        copy.start()
        sent.append(copy)

    project(lane_f, True)
    arrive(sibling)
    project(sibling)
    forward(0)
    forward(1)
    project(same[0])
    project(same[1])
    forward(2)
    project(same[2])
    for i in range(3):
        arrive(cross[i])
        project(cross[i])
    out_ref[...] = proj_v[...].astype(BF16)

    for copy in sent:
        copy.wait_send()
    for t in others:
        query_copy(t, me).wait_send()
        part_copy(t, me).wait_send()
        stat_copy(t, me).wait_send()


def body(
    queries, new_keys, new_values, prompt_keys, prompt_values, suffix_keys, suffix_values,
    suffix_len, prompt_of_row, partner, out_weight,
):
    smem = pl.BlockSpec(memory_space=pltpu.SMEM)
    anywhere = pl.BlockSpec(memory_space=pl.ANY)
    vm = pltpu.VMEM
    dma = pltpu.SemaphoreType.DMA
    rows = STEPS * ROWS
    projected = pl.pallas_call(
        kernel,
        out_shape=jax.ShapeDtypeStruct((rows, WIDTH), BF16),
        in_specs=[smem] * 3 + [anywhere] * 8,
        out_specs=pl.BlockSpec(memory_space=pltpu.VMEM),
        scratch_shapes=[
            vm((ROWS, SLOT, HD), BF16), vm((rows, HD), BF16), vm((rows, HD), BF16),
            vm((ROWS, SUFFIX, HD), BF16), vm((ROWS, SUFFIX, HD), BF16),
            vm((LENGTH, HD), BF16), vm((LENGTH, HD), BF16), vm((HD, LENGTH), BF16),
            vm((SUFS * WIDTH, WIDTH), BF16),
            vm((8, 128), jnp.int32), pltpu.SMEM((8, 128), jnp.int32),
            vm((OWNERS * BLOCK, HD), BF16), vm((OWNERS * BLOCK, HD), BF16),
            vm((2, SPAN, CHUNK), F32), vm((8, CHUNK), F32), vm((8, CHUNK), F32), vm((HD, CHUNK), F32),
            vm((OWNERS, CAP, SLOT, HD), BF16), vm((OWNERS, 8, BLOCK), F32),
            vm((OWNERS, CAP, SLOT, HD), BF16), vm((OWNERS, 8, BLOCK), F32),
            vm((CAP, SLOT, OWNERS * 8), F32),
            vm((ROWS * SLOT, rows), F32), vm((ROWS * SLOT, rows), BF16),
            vm((ROWS * SLOT, HD), F32), vm((ROWS * SLOT, HD), F32), vm((ROWS * SLOT, HD), F32),
            vm((ROWS * SLOT, HD), F32), vm((SUFS, ROWS * SLOT, HD), BF16), vm((rows, WIDTH), F32),
            dma((8,)), dma,
            dma((OWNERS,)), dma((OWNERS,)), dma((OWNERS,)), dma((OWNERS,)),
            dma((OWNERS,)), dma((OWNERS,)), dma((SUFS,)), dma((SUFS,)),
        ],
        compiler_params=pltpu.CompilerParams(
            collective_id=0, has_side_effects=True, vmem_limit_bytes=58 * 2**20
        ),
    )(
        prompt_of_row, partner, suffix_len,
        queries.reshape(ROWS, SLOT, HD), new_keys.reshape(rows, HD), new_values.reshape(rows, HD),
        suffix_keys, suffix_values,
        prompt_keys.reshape(LENGTH, HD), prompt_values.reshape(LENGTH, HD), out_weight,
    )
    return projected.reshape(ROWS, STEPS, WIDTH)


def solution(mesh):
    return jax.shard_map(
        body,
        mesh=mesh,
        in_specs=(
            P("owner", None, "suf"),
            P("owner", None, "suf"),
            P("owner", None, "suf"),
            P("owner", "suf", None, None),
            P("owner", "suf", None, None),
            P("owner", None, "suf"),
            P("owner", None, "suf"),
            P("owner"),
            P("owner"),
            P("owner"),
            P(None, "suf"),
        ),
        out_specs=P("owner", None, "suf"),
        check_vma=False,
    )
```

time: 208 us -> 60 us (0.29)
  matrix products: 61.4 us -> 0 us
  Pallas kernels: 0 us -> 56.6 us
  waiting for transfers between devices: 50.8 us -> 0 us
  local copies, waits for them, and re-layouts: 30.6 us -> 3.26 us
  other arithmetic: 21.9 us -> 0 us
  blocking collectives: 14.8 us -> 0 us
  between operations: 14.6 us -> 0.01 us
  starting transfers between devices: 11.9 us -> 0 us
    dot_general x25 -> x0, matrix products: 61.4 us -> none  [the longest x8 23.6 us: add_block(): jnp.einsum('kmgl,kld->kmgd', weights.astype(jnp.bfloat16), value_block, p...]
    pallas_call x0 -> x1, Pallas kernels: none -> 56.6 us  [body(): pl.pallas_call(kernel, out_shape=jax.ShapeDtypeStruct((rows, WIDTH), BF16...]
    all_gather x2 -> x0, waiting for transfers between devices: 41.5 us -> none  [the longest x1 29.1 us: body(): lax.all_gather(attention, 'suf', axis=1, tiled=True)]
    unnamed x1 -> x0, blocking collectives: 14.8 us -> none
    reduce_sum x11 -> x0, other arithmetic: 13.4 us -> none  [the longest x8 10.9 us: add_block(): weight_sum = weight_sum * decay + weights.sum(-1)]
    gather x9 -> x0, local copies, waits for them, and re-layouts: 12.6 us -> none  [the longest x1 3.9 us: body(): cache_values[parent_local]]
    all_to_all x3 -> x0, starting transfers between devices: 11.7 us -> none  [the longest x1 4.66 us: body(): lax.all_to_all(part_max, 'owner', split_axis=0, concat_axis=0, tiled=True)]
    unnamed x77 -> x0, local copies, waits for them, and re-layouts: 9.08 us -> none
  transfers between devices with their start and end apart: 5 -> 0, of which waited for: 4 -> 0; matrix products, arithmetic and copies ran while one was open for 17% -> 0% of each run, Pallas kernels for 0% -> 0%
where the time goes in v1:
time: 60 us; the launch traced here: 59.8 us
  Pallas kernels  56.6 us (94%)
  local copies, waits for them, and re-layouts  3.26 us (5%)
    pallas_call x1, Pallas kernels, body(): pl.pallas_call(kernel, out_shape=jax.ShapeDtypeStruct((rows, WIDTH), BF16...  56.6 us
    reshape x1, local copies, waits for them, and re-layouts, body(): queries.reshape(ROWS, SLOT, HD)  1.65 us
    reshape x1, local copies, waits for them, and re-layouts, body(): return projected.reshape(ROWS, STEPS, WIDTH)  1.61 us

profile of v1, /device:TPU:1, one launch (start us, length us, event | category | flops | bytes accessed | tf_op | source)
XLA Modules:
  0.0 59.8 jit_solution(16910035266176792756)
XLA Ops:
  0.0 1.6 %reshape.18.q_hbm = bf16[32,16,128]{2,1,0:T(8,128)(2,1)} reshape(bf16[32,2,1024]{2,1,0:T(2,128)(2,1)} %param.11) | data formatting | bytes 262144 | tf_op jit(solution)/shard_map/reshape | solution.py:385
  1.6 56.6 %shard_map.109 = bf16[64,1024]{1,0:T(8,128)(2,1)} custom-call(s32[32]{0:T(128)} %prompt_s.1, s32[32]{0:T(128)} %partner_s.1, s32[32]{0:T(128)} %length_s.1, bf16[32,16,128]{2,1,0:T(8,128)(2,1)} %reshape.18.q_hbm, bf16[64,128]{1,0:T(8,128)(2,1)} %bitcast.6, bf16[64,128]{1,0:T(8,128)(2,1)} %bitcast.7, bf16[32,256,128]{2,1,0:T(8,128)(2,1)} %ks_hbm.1, ...), custom_call_target="tpu_custom_call" | custom-call | tf_op jit(solution)/shard_map/pallas_call | solution.py:357
  58.2 1.6 %reshape.23 = bf16[32,2,1024]{2,1,0:T(2,128)(2,1)} reshape(bf16[64,1024]{1,0:T(8,128)(2,1)} %shard_map.109) | data formatting | bytes 262144 | tf_op jit(solution)/shard_map/reshape | solution.py:389

commit v2 on v1

v2 whole, which is shorter than its diff:
```python
import jax
import jax.numpy as jnp
from jax import lax
from jax.experimental import pallas as pl
from jax.experimental.pallas import tpu as pltpu
from jax.sharding import PartitionSpec as P

MESH = pl.DeviceIdType.MESH
HD = 128
GROUP = 8
CAP = 8
STEPS = 2
SIDE = 4
OWNERS = 16
SUFS = 8
ROWS = 32
SLOT = STEPS * GROUP
BLOCK = CAP * SLOT
LENGTH = 8192
SUFFIX = 256
WIDTH = GROUP * HD
SPAN = 1024
CHUNK = SIDE * BLOCK
SPANS = LENGTH // SPAN
HALF = GROUP // 2
RATE = HD ** (-0.5) * 1.4426950408889634
F32 = jnp.float32
BF16 = jnp.bfloat16


def dot_t(a, b):
    return lax.dot_general(a, b, (((1,), (1,)), ((), ())), preferred_element_type=F32)


STEPS_Y = (0, 0, 2, 2, 1, 1, 3, 3, 2, 2, 1, 3, 0, 0, 1, 3)
STEPS_Z = (0, 2, 0, 2, 1, 3, 1, 3, 1, 3, 2, 2, 1, 3, 0, 0)
OPPOSITE = (0, 1, 2, 3, 7, 6, 5, 4, 9, 8, 11, 10, 13, 12, 15, 14)


def kernel(
    prompt_s, partner_s, length_s,
    q_hbm, nk_hbm, nv_hbm, ks_hbm, vs_hbm, k_hbm, v_hbm, w_hbm,
    out_ref,
    q_v, nk_v, nv_v, ks_v, vs_v, k_v, v_v, vt_v, w_v,
    table_v, table_s, pack_v, rq_v,
    s_v, p_v, top_v, m_v, l_v, acc_v,
    part_v, stat_v, back_v, bstat_v, bstat_t,
    e_v, pe_v, lo_v, lm_v, ls_v,
    att_v, ag_v, proj_v,
    load_sem, table_sem,
    qsend, qrecv, bsend, brecv, ssend, srecv, gsend, grecv,
):
    me = lax.axis_index("owner")
    mine = lax.axis_index("suf")
    y, z = me // SIDE, me % SIDE
    x, core = mine // 2, mine % 2
    right, left = (x + 1) % SIDE * 2 + core, (x + 3) % SIDE * 2 + core
    across = (x + 2) % SIDE * 2 + core
    sibling = x * 2 + 1 - core

    def owner_at(dy, dz):
        return (y + dy) % SIDE * SIDE + (z + dz) % SIDE

    others = [(i, owner_at(STEPS_Y[i], STEPS_Z[i])) for i in range(1, OWNERS)]

    barrier = pltpu.get_barrier_semaphore()
    for _, t in others:
        pl.semaphore_signal(barrier, inc=1, device_id={"owner": t}, device_id_type=MESH)
    for t in (right, left, sibling):
        pl.semaphore_signal(barrier, inc=1, device_id={"suf": t}, device_id_type=MESH)

    pairs = (
        (q_hbm, q_v), (nk_hbm, nk_v), (nv_hbm, nv_v), (ks_hbm, ks_v), (vs_hbm, vs_v),
        (v_hbm, v_v), (k_hbm, k_v), (w_hbm, w_v),
    )
    loads = [
        pltpu.make_async_copy(src, dst, load_sem.at[i]) for i, (src, dst) in enumerate(pairs)
    ]
    for copy in loads:
        copy.start()
    ld_q, ld_nk, ld_nv, ld_ks, ld_vs, ld_v, ld_k, ld_w = loads

    lane = lax.broadcasted_iota(jnp.int32, (8, 128), 1)
    sub = lax.broadcasted_iota(jnp.int32, (8, 128), 0)
    lane_prompt, lane_place = lane // CAP, lane % CAP
    count = jnp.zeros((8, 128), jnp.int32)
    row_of = jnp.zeros((8, 128), jnp.int32)
    own_prompt = jnp.zeros((8, 128), jnp.int32)
    for r in range(ROWS):
        named = prompt_s[r]
        match = lane_prompt == named
        row_of = jnp.where(match & (count == lane_place), r, row_of)
        count = count + jnp.where(match, 1, 0)
        own_prompt = jnp.where(lane == r, named, own_prompt)
    rank = jnp.zeros((8, 128), jnp.int32)
    for r in range(ROWS):
        rank = rank + jnp.where((own_prompt == prompt_s[r]) & (lane > r), 1, 0)
    table_v[...] = jnp.where(sub == 0, row_of, rank % CAP)
    to_smem = pltpu.make_async_copy(table_v, table_s, table_sem)
    to_smem.start()
    to_smem.wait()
    ld_q.wait()

    def pack(i, carry):
        for u in range(8):
            slot = i * 8 + u
            pack_v[pl.ds(pl.multiple_of(slot * SLOT, SLOT), SLOT), :] = q_v[table_s[0, slot]]
        return carry

    lax.fori_loop(0, OWNERS * CAP // 8, pack, 0)

    def block_of(i):
        return pl.ds(pl.multiple_of(i * BLOCK, BLOCK), BLOCK)

    pl.semaphore_wait(barrier, OWNERS - 1 + 3)

    def query_copy(t, i, there):
        return pltpu.make_async_remote_copy(
            src_ref=pack_v.at[block_of(t)], dst_ref=rq_v.at[block_of(there)],
            send_sem=qsend.at[i], recv_sem=qrecv.at[there],
            device_id={"owner": t}, device_id_type=MESH,
        )

    for i, t in others:
        query_copy(t, i, OPPOSITE[i]).start()
    rq_v[block_of(0), :] = pack_v[block_of(me), :]

    ld_nk.wait()
    ld_nv.wait()
    e_v[...] = dot_t(q_v[...].reshape(ROWS * SLOT, HD), nk_v[...])
    ld_ks.wait()
    ld_vs.wait()
    early = lax.broadcasted_iota(jnp.int32, (SLOT, SUFFIX), 0) % STEPS == 0
    slot_lane = lax.broadcasted_iota(jnp.int32, (SLOT, SUFFIX), 1)
    extra_early = lax.broadcasted_iota(jnp.int32, (SLOT, 2 * ROWS), 0) % STEPS == 0
    extra_lane = lax.broadcasted_iota(jnp.int32, (SLOT, 2 * ROWS), 1)
    part_early = lax.broadcasted_iota(jnp.int32, (SLOT, HD), 0) % STEPS == 0

    def local_row(r):
        parent = partner_s[r] % ROWS
        rows = pl.ds(pl.multiple_of(r * SLOT, SLOT), SLOT)
        query = q_v[r]
        scores = jnp.where(early, dot_t(query, ks_v[r]), dot_t(query, ks_v[parent]))
        valid = slot_lane < jnp.where(early, length_s[r], length_s[parent])
        scores = jnp.where(valid, scores, -1e30)
        extra = e_v[rows, :]
        one = jnp.where(extra_early, 2 * r, 2 * parent)
        two = jnp.where(extra_early, 2 * r, 2 * r + 1)
        extra_valid = (extra_lane == one) | (extra_lane == two)
        extra = jnp.where(extra_valid, extra, -1e30)
        top = jnp.maximum(
            jnp.max(scores, axis=1, keepdims=True), jnp.max(extra, axis=1, keepdims=True)
        )
        weights = jnp.where(valid, jnp.exp2((scores - top) * RATE), 0.0)
        extra = jnp.where(extra_valid, jnp.exp2((extra - top) * RATE), 0.0)
        total = jnp.sum(weights, axis=1, keepdims=True) + jnp.sum(extra, axis=1, keepdims=True)
        weights = weights.astype(BF16)
        first = jnp.dot(weights, vs_v[r], preferred_element_type=F32)
        second = jnp.dot(weights, vs_v[parent], preferred_element_type=F32)
        lo_v[rows, :] = jnp.where(part_early, first, second)
        pe_v[rows, :] = extra.astype(BF16)
        lm_v[rows, :] = jnp.broadcast_to(top, (SLOT, HD))
        ls_v[rows, :] = jnp.broadcast_to(total, (SLOT, HD))

    def local_rows(i, carry):
        for u in range(4):
            local_row(i * 4 + u)
        return carry

    lax.fori_loop(0, ROWS // 4, local_rows, 0)
    lo_v[...] += jnp.dot(pe_v[...], nv_v[...], preferred_element_type=F32)

    ld_v.wait()

    def turn(i, carry):
        at = pl.ds(pl.multiple_of(i * 512, 512), 512)
        vt_v[:, at] = v_v[at, :].T
        return carry

    lax.fori_loop(0, LENGTH // 512, turn, 0)
    ld_k.wait()
    for i in range(1, 2 * SIDE):
        query_copy(others[0][1], i, i).wait_recv()

    def score(c, j):
        at = pl.ds(pl.multiple_of(c * CHUNK, CHUNK), CHUNK)
        s = dot_t(k_v[j * SPAN:(j + 1) * SPAN, :], rq_v[at, :])
        s_v[j % 2] = s
        top_v[j % 2] = jnp.max(s.reshape(SPAN // 8, 8, CHUNK), axis=0)

    def absorb(j):
        top = jnp.max(top_v[j % 2], axis=0, keepdims=True)
        if j == 0:
            m_new = jnp.broadcast_to(top, (8, CHUNK))
        else:
            m_old = m_v[...]
            m_new = jnp.maximum(m_old, top)
            decay = jnp.exp2((m_old - m_new) * RATE)
        m_v[...] = m_new
        p = jnp.exp2((s_v[j % 2] - m_new[:1]) * RATE)
        total = jnp.sum(p.reshape(SPAN // 8, 8, CHUNK), axis=0)
        p_v[...] = p.astype(BF16)
        term = jnp.dot(
            vt_v[:, j * SPAN:(j + 1) * SPAN], p_v[...], preferred_element_type=F32
        )
        if j == 0:
            l_v[...] = total
            acc_v[...] = term
        else:
            l_v[...] = l_v[...] * decay + total
            acc_v[...] = acc_v[...] * decay[:1] + term

    def part_copy(i, t, source):
        return pltpu.make_async_remote_copy(
            src_ref=part_v.at[i], dst_ref=back_v.at[source],
            send_sem=bsend.at[i], recv_sem=brecv.at[source],
            device_id={"owner": t}, device_id_type=MESH,
        )

    def stat_copy(i, t, source):
        return pltpu.make_async_remote_copy(
            src_ref=stat_v.at[i], dst_ref=bstat_v.at[source],
            send_sem=ssend.at[i], recv_sem=srecv.at[source],
            device_id={"owner": t}, device_id_type=MESH,
        )

    def pick(table, c, k):
        value = table[k]
        for n in range(1, SIDE):
            value = jnp.where(c == n, table[n * SIDE + k], value)
        return value

    score(0, 0)

    def chunk(c, carry):
        @pl.when((c > 0) & (c < SIDE - 1))
        def _():
            for k in range(SIDE):
                query_copy(others[0][1], (c + 1) * SIDE + k, (c + 1) * SIDE + k).wait_recv()

        for j in range(SPANS):
            if j + 1 < SPANS:
                score(c, j + 1)
            else:
                score(jnp.minimum(c + 1, SIDE - 1), 0)
            absorb(j)
        total = jnp.sum(l_v[...], axis=0, keepdims=True)
        top = m_v[:1, :]
        done = acc_v[...] / total
        for k in range(SIDE):
            i = c * SIDE + k
            t = owner_at(pick(STEPS_Y, c, k), pick(STEPS_Z, c, k))
            cols = slice(k * BLOCK, (k + 1) * BLOCK)
            piece = done[:, cols].T.astype(BF16).reshape(CAP, SLOT, HD)
            stats = jnp.concatenate(
                [top[:, cols], total[:, cols], jnp.zeros((6, BLOCK), F32)], axis=0
            )

            @pl.when(i == 0)
            def _():
                back_v[me] = piece
                bstat_v[me] = stats

            @pl.when(i != 0)
            def _():
                part_v[i] = piece
                stat_v[i] = stats
                part_copy(i, t, me).start()
                stat_copy(i, t, me).start()

        return carry

    lax.fori_loop(0, SIDE, chunk, 0)

    for i, t in others:
        part_copy(i, t, t).wait_recv()
        stat_copy(i, t, t).wait_recv()

    bstat_t[...] = bstat_v[...].reshape(OWNERS * 8, BLOCK).T.reshape(CAP, SLOT, OWNERS * 8)
    stat_lane = lax.broadcasted_iota(jnp.int32, (SLOT, OWNERS * 8), 1)

    def merge_row(r):
        named = prompt_s[r]
        rows = pl.ds(pl.multiple_of(r * SLOT, SLOT), SLOT)
        place = table_s[1, r]
        part = back_v[named, place].astype(F32)
        both = bstat_t[place]
        p_max = jnp.sum(jnp.where(stat_lane == named * 8, both, 0.0), axis=1, keepdims=True)
        p_sum = jnp.sum(jnp.where(stat_lane == named * 8 + 1, both, 0.0), axis=1, keepdims=True)
        l_max, l_sum = lm_v[rows, :], ls_v[rows, :]
        top = jnp.maximum(p_max, l_max)
        a = p_sum * jnp.exp2((p_max - top) * RATE)
        b = jnp.exp2((l_max - top) * RATE)
        att_v[rows, :] = (a * part + b * lo_v[rows, :]) / (a + b * l_sum)

    for r in range(ROWS):
        merge_row(r)
    for h in range(GROUP):
        both = [att_v[pl.ds(STEPS * h + s, ROWS, stride=SLOT), :] for s in range(STEPS)]
        ag_v[mine, h // HALF, h % HALF] = jnp.concatenate(both, axis=0).astype(BF16)

    sent = []

    def gather_copy(block, half, to, i):
        return pltpu.make_async_remote_copy(
            src_ref=ag_v.at[block, half], dst_ref=ag_v.at[block, half],
            send_sem=gsend.at[i], recv_sem=grecv.at[block, half],
            device_id={"suf": to}, device_id_type=MESH,
        )

    def send(block, half, to):
        copy = gather_copy(block, half, to, len(sent))
        copy.start()
        sent.append(copy)

    def arrive(block, half):
        gather_copy(block, half, sibling, 0).wait_recv()

    def project(block, half, first=False):
        a = ag_v[block, half]
        a = jnp.concatenate([a[h] for h in range(HALF)], axis=1)
        start = block * WIDTH + half * HALF * HD
        w = w_v[pl.ds(pl.multiple_of(start, HALF * HD), HALF * HD), :]
        term = jnp.dot(a, w, preferred_element_type=F32)
        if first:
            proj_v[...] = term
        else:
            proj_v[...] += term

    send(mine, 0, right)
    send(mine, 1, left)
    send(mine, 1, right)
    send(mine, 0, left)
    send(mine, 0, sibling)
    send(mine, 1, sibling)
    ld_w.wait()
    project(mine, 0, True)
    project(mine, 1)
    arrive(left, 0)
    send(left, 0, right)
    send(left, 0, sibling)
    arrive(right, 1)
    send(right, 1, left)
    send(right, 1, sibling)
    for half in range(2):
        arrive(sibling, half)
        project(sibling, half)
    project(left, 0)
    project(right, 1)
    for block, half in ((left, 1), (right, 0)):
        arrive(block, half)
        send(block, half, sibling)
    project(left, 1)
    project(right, 0)
    for half in range(2):
        arrive(across, half)
        send(across, half, sibling)
    project(across, 0)
    project(across, 1)
    turned = 1 - 2 * core
    for block, half in (
        (left, 0), (right, 1), (left, 1), (right, 0), (across, 0), (across, 1),
    ):
        arrive(block + turned, half)
        project(block + turned, half)

    for j in range(GROUP):
        for s in range(STEPS):
            att_v[pl.ds(STEPS * j + s, ROWS, stride=SLOT), :] = (
                proj_v[s * ROWS:(s + 1) * ROWS, j * HD:(j + 1) * HD]
            )
    out_ref[...] = att_v[...].astype(BF16).reshape(ROWS, SLOT, HD)

    for copy in sent:
        copy.wait_send()
    for i, t in others:
        query_copy(t, i, OPPOSITE[i]).wait_send()
        part_copy(i, t, me).wait_send()
        stat_copy(i, t, me).wait_send()


def body(
    queries, new_keys, new_values, prompt_keys, prompt_values, suffix_keys, suffix_values,
    suffix_len, prompt_of_row, partner, out_weight,
):
    smem = pl.BlockSpec(memory_space=pltpu.SMEM)
    anywhere = pl.BlockSpec(memory_space=pl.ANY)
    vm = pltpu.VMEM
    dma = pltpu.SemaphoreType.DMA
    rows = STEPS * ROWS
    projected = pl.pallas_call(
        kernel,
        out_shape=jax.ShapeDtypeStruct((ROWS, SLOT, HD), BF16),
        in_specs=[smem] * 3 + [anywhere] * 8,
        out_specs=pl.BlockSpec(memory_space=pltpu.VMEM),
        scratch_shapes=[
            vm((ROWS, SLOT, HD), BF16), vm((rows, HD), BF16), vm((rows, HD), BF16),
            vm((ROWS, SUFFIX, HD), BF16), vm((ROWS, SUFFIX, HD), BF16),
            vm((LENGTH, HD), BF16), vm((LENGTH, HD), BF16), vm((HD, LENGTH), BF16),
            vm((SUFS * WIDTH, WIDTH), BF16),
            vm((8, 128), jnp.int32), pltpu.SMEM((8, 128), jnp.int32),
            vm((OWNERS * BLOCK, HD), BF16), vm((OWNERS * BLOCK, HD), BF16),
            vm((2, SPAN, CHUNK), F32), vm((SPAN, CHUNK), BF16), vm((2, 8, CHUNK), F32),
            vm((8, CHUNK), F32), vm((8, CHUNK), F32), vm((HD, CHUNK), F32),
            vm((OWNERS, CAP, SLOT, HD), BF16), vm((OWNERS, 8, BLOCK), F32),
            vm((OWNERS, CAP, SLOT, HD), BF16), vm((OWNERS, 8, BLOCK), F32),
            vm((CAP, SLOT, OWNERS * 8), F32),
            vm((ROWS * SLOT, rows), F32), vm((ROWS * SLOT, rows), BF16),
            vm((ROWS * SLOT, HD), F32), vm((ROWS * SLOT, HD), F32), vm((ROWS * SLOT, HD), F32),
            vm((ROWS * SLOT, HD), F32), vm((SUFS, 2, HALF, rows, HD), BF16), vm((rows, WIDTH), F32),
            dma((8,)), dma,
            dma((OWNERS,)), dma((OWNERS,)), dma((OWNERS,)), dma((OWNERS,)),
            dma((OWNERS,)), dma((OWNERS,)), dma((14,)), dma((SUFS, 2)),
        ],
        compiler_params=pltpu.CompilerParams(
            collective_id=0, has_side_effects=True, vmem_limit_bytes=58 * 2**20
        ),
    )(
        prompt_of_row, partner, suffix_len,
        queries.reshape(ROWS, STEPS, GROUP, HD).swapaxes(1, 2).reshape(ROWS, SLOT, HD), new_keys.reshape(rows, HD), new_values.reshape(rows, HD),
        suffix_keys, suffix_values,
        prompt_keys.reshape(LENGTH, HD), prompt_values.reshape(LENGTH, HD), out_weight,
    )
    projected = projected.reshape(ROWS, GROUP, STEPS, HD).swapaxes(1, 2)
    return projected.reshape(ROWS, STEPS, WIDTH)


def solution(mesh):
    return jax.shard_map(
        body,
        mesh=mesh,
        in_specs=(
            P("owner", None, "suf"),
            P("owner", None, "suf"),
            P("owner", None, "suf"),
            P("owner", "suf", None, None),
            P("owner", "suf", None, None),
            P("owner", None, "suf"),
            P("owner", None, "suf"),
            P("owner"),
            P("owner"),
            P("owner"),
            P(None, "suf"),
        ),
        out_specs=P("owner", None, "suf"),
        check_vma=False,
    )
```

time: 60 us -> 56.2 us (0.937)
  Pallas kernels: 56.6 us -> 54.4 us
  local copies, waits for them, and re-layouts: 3.26 us -> 1.65 us
    reshape x2 -> x0, local copies, waits for them, and re-layouts: 3.26 us -> none  [the longest x1 1.65 us: body(): queries.reshape(ROWS, SLOT, HD)]
    pallas_call x1, Pallas kernels: 56.6 us -> 54.4 us  [body(): pl.pallas_call(kernel, out_shape=jax.ShapeDtypeStruct((ROWS, SLOT, HD), B...]
    unnamed x0 -> x1, local copies, waits for them, and re-layouts: none -> 1.65 us
where the time goes in v2:
time: 56.2 us; the launch traced here: 56.1 us
  Pallas kernels  54.4 us (97%)
  local copies, waits for them, and re-layouts  1.65 us (3%)
    pallas_call x1, Pallas kernels, body(): pl.pallas_call(kernel, out_shape=jax.ShapeDtypeStruct((ROWS, SLOT, HD), B...  54.4 us
    unnamed x1, local copies, waits for them, and re-layouts  1.65 us

profile of v2, /device:TPU:1, one launch (start us, length us, event | category | flops | bytes accessed | tf_op | source)
XLA Modules:
  0.0 56.1 jit_solution(15321439737540607027)
XLA Ops:
  0.0 54.4 %shard_map.109 = bf16[32,16,128]{2,1,0:T(8,128)(2,1)} custom-call(s32[32]{0:T(128)} %prompt_s.1, s32[32]{0:T(128)} %partner_s.1, s32[32]{0:T(128)} %length_s.1, bf16[32,16,128]{2,1,0:T(8,128)(2,1)} %bitcast.17, bf16[64,128]{1,0:T(8,128)(2,1)} %bitcast.18, bf16[64,128]{1,0:T(8,128)(2,1)} %bitcast.19, bf16[32,256,128]{2,1,0:T(8,128)(2,1)} %ks_hbm.1, ...), custom_call_target="tpu_custom_call" | custom-call | tf_op jit(solution)/shard_map/pallas_call | solution.py:391
  54.4 1.7 %copy.15 = bf16[32,2,1024]{2,1,0:T(2,128)(2,1)} copy(bf16[32,2,1024]{2,1,0:T(2,128)(2,1)} %bitcast.16) | data formatting | bytes 262144

commit v3 on v2

--- a/solution.py
+++ b/solution.py
@@ -22,7 +22,8 @@
 SPAN = 1024
 CHUNK = SIDE * BLOCK
 SPANS = LENGTH // SPAN
-HALF = GROUP // 2
+PIECES = 4
+HEADS = GROUP // PIECES
 RATE = HD ** (-0.5) * 1.4426950408889634
 F32 = jnp.float32
 BF16 = jnp.bfloat16
@@ -45,7 +46,7 @@
     table_v, table_s, pack_v, rq_v,
     s_v, p_v, top_v, m_v, l_v, acc_v,
     part_v, stat_v, back_v, bstat_v, bstat_t,
-    e_v, pe_v, lo_v, lm_v, ls_v,
+    e_v, pe_v, ls_v, lw_v, lo_v, lm_v, lt_v,
     att_v, ag_v, proj_v,
     load_sem, table_sem,
     qsend, qrecv, bsend, brecv, ssend, srecv, gsend, grecv,
@@ -136,38 +137,52 @@
     extra_lane = lax.broadcasted_iota(jnp.int32, (SLOT, 2 * ROWS), 1)
     part_early = lax.broadcasted_iota(jnp.int32, (SLOT, HD), 0) % STEPS == 0
 
-    def local_row(r):
+    def local_scores(r):
         parent = partner_s[r] % ROWS
         rows = pl.ds(pl.multiple_of(r * SLOT, SLOT), SLOT)
         query = q_v[r]
         scores = jnp.where(early, dot_t(query, ks_v[r]), dot_t(query, ks_v[parent]))
         valid = slot_lane < jnp.where(early, length_s[r], length_s[parent])
-        scores = jnp.where(valid, scores, -1e30)
-        extra = e_v[rows, :]
+        ls_v[rows, :] = jnp.where(valid, scores, -1e30)
         one = jnp.where(extra_early, 2 * r, 2 * parent)
         two = jnp.where(extra_early, 2 * r, 2 * r + 1)
         extra_valid = (extra_lane == one) | (extra_lane == two)
-        extra = jnp.where(extra_valid, extra, -1e30)
+        e_v[rows, :] = jnp.where(extra_valid, e_v[rows, :], -1e30)
+
+    def local_weights(i):
+        rows = pl.ds(pl.multiple_of(i * BLOCK, BLOCK), BLOCK)
+        scores, extra = ls_v[rows, :], e_v[rows, :]
         top = jnp.maximum(
             jnp.max(scores, axis=1, keepdims=True), jnp.max(extra, axis=1, keepdims=True)
         )
-        weights = jnp.where(valid, jnp.exp2((scores - top) * RATE), 0.0)
-        extra = jnp.where(extra_valid, jnp.exp2((extra - top) * RATE), 0.0)
+        weights = jnp.exp2((scores - top) * RATE)
+        extra = jnp.exp2((extra - top) * RATE)
         total = jnp.sum(weights, axis=1, keepdims=True) + jnp.sum(extra, axis=1, keepdims=True)
-        weights = weights.astype(BF16)
+        lw_v[rows, :] = weights.astype(BF16)
+        pe_v[rows, :] = extra.astype(BF16)
+        lm_v[rows, :] = jnp.broadcast_to(top, (BLOCK, HD))
+        lt_v[rows, :] = jnp.broadcast_to(total, (BLOCK, HD))
+
+    def local_values(r):
+        parent = partner_s[r] % ROWS
+        rows = pl.ds(pl.multiple_of(r * SLOT, SLOT), SLOT)
+        weights = lw_v[rows, :]
         first = jnp.dot(weights, vs_v[r], preferred_element_type=F32)
         second = jnp.dot(weights, vs_v[parent], preferred_element_type=F32)
         lo_v[rows, :] = jnp.where(part_early, first, second)
-        pe_v[rows, :] = extra.astype(BF16)
-        lm_v[rows, :] = jnp.broadcast_to(top, (SLOT, HD))
-        ls_v[rows, :] = jnp.broadcast_to(total, (SLOT, HD))
-
-    def local_rows(i, carry):
-        for u in range(4):
-            local_row(i * 4 + u)
-        return carry
-
-    lax.fori_loop(0, ROWS // 4, local_rows, 0)
+
+    def by_eight(step):
+        def run(i, carry):
+            for u in range(8):
+                step(i * 8 + u)
+            return carry
+
+        lax.fori_loop(0, ROWS // 8, run, 0)
+
+    by_eight(local_scores)
+    for i in range(ROWS * SLOT // BLOCK):
+        local_weights(i)
+    by_eight(local_values)
     lo_v[...] += jnp.dot(pe_v[...], nv_v[...], preferred_element_type=F32)
 
     ld_v.wait()
@@ -287,7 +302,7 @@
         both = bstat_t[place]
         p_max = jnp.sum(jnp.where(stat_lane == named * 8, both, 0.0), axis=1, keepdims=True)
         p_sum = jnp.sum(jnp.where(stat_lane == named * 8 + 1, both, 0.0), axis=1, keepdims=True)
-        l_max, l_sum = lm_v[rows, :], ls_v[rows, :]
+        l_max, l_sum = lm_v[rows, :], lt_v[rows, :]
         top = jnp.maximum(p_max, l_max)
         a = p_sum * jnp.exp2((p_max - top) * RATE)
         b = jnp.exp2((l_max - top) * RATE)
@@ -295,74 +310,94 @@
 
     for r in range(ROWS):
         merge_row(r)
-    for h in range(GROUP):
-        both = [att_v[pl.ds(STEPS * h + s, ROWS, stride=SLOT), :] for s in range(STEPS)]
-        ag_v[mine, h // HALF, h % HALF] = jnp.concatenate(both, axis=0).astype(BF16)
-
     sent = []
 
-    def gather_copy(block, half, to, i):
+    def gather_copy(block, piece, to, i):
         return pltpu.make_async_remote_copy(
-            src_ref=ag_v.at[block, half], dst_ref=ag_v.at[block, half],
-            send_sem=gsend.at[i], recv_sem=grecv.at[block, half],
+            src_ref=ag_v.at[block, piece], dst_ref=ag_v.at[block, piece],
+            send_sem=gsend.at[i], recv_sem=grecv.at[block, piece],
             device_id={"suf": to}, device_id_type=MESH,
         )
 
-    def send(block, half, to):
-        copy = gather_copy(block, half, to, len(sent))
+    def send(block, piece, to):
+        copy = gather_copy(block, piece, to, len(sent))
         copy.start()
         sent.append(copy)
 
-    def arrive(block, half):
-        gather_copy(block, half, sibling, 0).wait_recv()
-
-    def project(block, half, first=False):
-        a = ag_v[block, half]
-        a = jnp.concatenate([a[h] for h in range(HALF)], axis=1)
-        start = block * WIDTH + half * HALF * HD
-        w = w_v[pl.ds(pl.multiple_of(start, HALF * HD), HALF * HD), :]
+    def arrive(block, piece):
+        gather_copy(block, piece, sibling, 0).wait_recv()
+
+    def project(block, piece, first=False):
+        a = ag_v[block, piece]
+        a = jnp.concatenate([a[h] for h in range(HEADS)], axis=1)
+        start = block * WIDTH + piece * HEADS * HD
+        w = w_v[pl.ds(pl.multiple_of(start, HEADS * HD), HEADS * HD), :]
         term = jnp.dot(a, w, preferred_element_type=F32)
         if first:
             proj_v[...] = term
         else:
             proj_v[...] += term
 
-    send(mine, 0, right)
-    send(mine, 1, left)
-    send(mine, 1, right)
-    send(mine, 0, left)
-    send(mine, 0, sibling)
-    send(mine, 1, sibling)
+    def ready(piece):
+        for h in range(piece * HEADS, (piece + 1) * HEADS):
+            both = [att_v[pl.ds(STEPS * h + s, ROWS, stride=SLOT), :] for s in range(STEPS)]
+            ag_v[mine, piece, h % HEADS] = jnp.concatenate(both, axis=0).astype(BF16)
+
+    middle = PIECES // 2
+    for p in range(middle):
+        ready(p)
+        send(mine, p, right)
+        ready(middle + p)
+        send(mine, middle + p, left)
+    for p in range(middle):
+        send(mine, middle + p, right)
+        send(mine, p, left)
+    for p in range(PIECES):
+        send(mine, p, sibling)
     ld_w.wait()
-    project(mine, 0, True)
-    project(mine, 1)
-    arrive(left, 0)
-    send(left, 0, right)
-    send(left, 0, sibling)
-    arrive(right, 1)
-    send(right, 1, left)
-    send(right, 1, sibling)
-    for half in range(2):
-        arrive(sibling, half)
-        project(sibling, half)
-    project(left, 0)
-    project(right, 1)
-    for block, half in ((left, 1), (right, 0)):
-        arrive(block, half)
-        send(block, half, sibling)
-    project(left, 1)
-    project(right, 0)
-    for half in range(2):
-        arrive(across, half)
-        send(across, half, sibling)
-    project(across, 0)
-    project(across, 1)
+    for p in range(PIECES):
+        project(mine, p, p == 0)
+    for p in range(middle):
+        arrive(left, p)
+        send(left, p, right)
+        send(left, p, sibling)
+        arrive(right, middle + p)
+        send(right, middle + p, left)
+        send(right, middle + p, sibling)
+    for p in range(PIECES):
+        arrive(sibling, p)
+        project(sibling, p)
+    for p in range(middle):
+        project(left, p)
+        project(right, middle + p)
+    for p in range(middle):
+        arrive(left, middle + p)
+        send(left, middle + p, sibling)
+        arrive(right, p)
+        send(right, p, sibling)
+    for p in range(middle):
+        project(left, middle + p)
+        project(right, p)
+    for p in range(middle):
+        arrive(across, p)
+        send(across, p, sibling)
+        arrive(across, middle + p)
+        send(across, middle + p, sibling)
+    for p in range(PIECES):
+        project(across, p)
     turned = 1 - 2 * core
-    for block, half in (
-        (left, 0), (right, 1), (left, 1), (right, 0), (across, 0), (across, 1),
-    ):
-        arrive(block + turned, half)
-        project(block + turned, half)
+    for p in range(middle):
+        for block, piece in ((left, p), (right, middle + p)):
+            arrive(block + turned, piece)
+            project(block + turned, piece)
+    for p in range(middle):
+        for block, piece in ((left, middle + p), (right, p)):
+            arrive(block + turned, piece)
+            project(block + turned, piece)
+    for p in range(middle):
+        for piece in (p, middle + p):
+            arrive(across + turned, piece)
+            project(across + turned, piece)
 
     for j in range(GROUP):
         for s in range(STEPS):
@@ -406,11 +441,12 @@
             vm((OWNERS, CAP, SLOT, HD), BF16), vm((OWNERS, 8, BLOCK), F32),
             vm((CAP, SLOT, OWNERS * 8), F32),
             vm((ROWS * SLOT, rows), F32), vm((ROWS * SLOT, rows), BF16),
+            vm((ROWS * SLOT, SUFFIX), F32), vm((ROWS * SLOT, SUFFIX), BF16),
             vm((ROWS * SLOT, HD), F32), vm((ROWS * SLOT, HD), F32), vm((ROWS * SLOT, HD), F32),
-            vm((ROWS * SLOT, HD), F32), vm((SUFS, 2, HALF, rows, HD), BF16), vm((rows, WIDTH), F32),
+            vm((ROWS * SLOT, HD), F32), vm((SUFS, PIECES, HEADS, rows, HD), BF16), vm((rows, WIDTH), F32),
             dma((8,)), dma,
             dma((OWNERS,)), dma((OWNERS,)), dma((OWNERS,)), dma((OWNERS,)),
-            dma((OWNERS,)), dma((OWNERS,)), dma((14,)), dma((SUFS, 2)),
+            dma((OWNERS,)), dma((OWNERS,)), dma((7 * PIECES,)), dma((SUFS, PIECES)),
         ],
         compiler_params=pltpu.CompilerParams(
             collective_id=0, has_side_effects=True, vmem_limit_bytes=58 * 2**20

time: 56.2 us -> 52.3 us (0.931)
  Pallas kernels: 54.4 us -> 50.5 us
    pallas_call x1, Pallas kernels: 54.4 us -> 50.5 us  [body(): pl.pallas_call(kernel, out_shape=jax.ShapeDtypeStruct((ROWS, SLOT, HD), B...]
where the time goes in v3:
time: 52.3 us; the launch traced here: 52.2 us
  Pallas kernels  50.5 us (97%)
  local copies, waits for them, and re-layouts  1.65 us (3%)
    pallas_call x1, Pallas kernels, body(): pl.pallas_call(kernel, out_shape=jax.ShapeDtypeStruct((ROWS, SLOT, HD), B...  50.5 us
    unnamed x1, local copies, waits for them, and re-layouts  1.65 us

profile of v3, /device:TPU:1, one launch (start us, length us, event | category | flops | bytes accessed | tf_op | source)
XLA Modules:
  0.0 52.2 jit_solution(2940130367067911336)
XLA Ops:
  0.0 50.5 %shard_map.109 = bf16[32,16,128]{2,1,0:T(8,128)(2,1)} custom-call(s32[32]{0:T(128)} %prompt_s.1, s32[32]{0:T(128)} %partner_s.1, s32[32]{0:T(128)} %length_s.1, bf16[32,16,128]{2,1,0:T(8,128)(2,1)} %bitcast.17, bf16[64,128]{1,0:T(8,128)(2,1)} %bitcast.18, bf16[64,128]{1,0:T(8,128)(2,1)} %bitcast.19, bf16[32,256,128]{2,1,0:T(8,128)(2,1)} %ks_hbm.1, ...), custom_call_target="tpu_custom_call" | custom-call | tf_op jit(solution)/shard_map/pallas_call | solution.py:426
  50.5 1.7 %copy.15 = bf16[32,2,1024]{2,1,0:T(2,128)(2,1)} copy(bf16[32,2,1024]{2,1,0:T(2,128)(2,1)} %bitcast.16) | data formatting | bytes 262144

commit v4 on v3

--- a/solution.py
+++ b/solution.py
@@ -33,9 +33,9 @@
     return lax.dot_general(a, b, (((1,), (1,)), ((), ())), preferred_element_type=F32)
 
 
-STEPS_Y = (0, 0, 2, 2, 1, 1, 3, 3, 2, 2, 1, 3, 0, 0, 1, 3)
-STEPS_Z = (0, 2, 0, 2, 1, 3, 1, 3, 1, 3, 2, 2, 1, 3, 0, 0)
-OPPOSITE = (0, 1, 2, 3, 7, 6, 5, 4, 9, 8, 11, 10, 13, 12, 15, 14)
+STEPS_Y = (0, 0, 1, 3, 2, 2, 1, 3, 2, 2, 1, 3, 0, 0, 1, 3)
+STEPS_Z = (0, 2, 1, 3, 1, 3, 3, 1, 0, 2, 2, 2, 1, 3, 0, 0)
+OPPOSITE = (0, 1, 3, 2, 5, 4, 7, 6, 8, 9, 11, 10, 13, 12, 15, 14)
 
 
 def kernel(
@@ -102,13 +102,10 @@
     to_smem.wait()
     ld_q.wait()
 
-    def pack(i, carry):
-        for u in range(8):
-            slot = i * 8 + u
+    def pack(t):
+        for u in range(CAP):
+            slot = t * CAP + u
             pack_v[pl.ds(pl.multiple_of(slot * SLOT, SLOT), SLOT), :] = q_v[table_s[0, slot]]
-        return carry
-
-    lax.fori_loop(0, OWNERS * CAP // 8, pack, 0)
 
     def block_of(i):
         return pl.ds(pl.multiple_of(i * BLOCK, BLOCK), BLOCK)
@@ -123,7 +120,9 @@
         )
 
     for i, t in others:
+        pack(t)
         query_copy(t, i, OPPOSITE[i]).start()
+    pack(me)
     rq_v[block_of(0), :] = pack_v[block_of(me), :]
 
     ld_nk.wait()
@@ -401,10 +400,9 @@
 
     for j in range(GROUP):
         for s in range(STEPS):
-            att_v[pl.ds(STEPS * j + s, ROWS, stride=SLOT), :] = (
+            out_ref[pl.ds(STEPS * j + s, ROWS, stride=SLOT), :] = (
                 proj_v[s * ROWS:(s + 1) * ROWS, j * HD:(j + 1) * HD]
             )
-    out_ref[...] = att_v[...].astype(BF16).reshape(ROWS, SLOT, HD)
 
     for copy in sent:
         copy.wait_send()
@@ -425,7 +423,7 @@
     rows = STEPS * ROWS
     projected = pl.pallas_call(
         kernel,
-        out_shape=jax.ShapeDtypeStruct((ROWS, SLOT, HD), BF16),
+        out_shape=jax.ShapeDtypeStruct((ROWS * SLOT, HD), F32),
         in_specs=[smem] * 3 + [anywhere] * 8,
         out_specs=pl.BlockSpec(memory_space=pltpu.VMEM),
         scratch_shapes=[
@@ -457,7 +455,7 @@
         suffix_keys, suffix_values,
         prompt_keys.reshape(LENGTH, HD), prompt_values.reshape(LENGTH, HD), out_weight,
     )
-    projected = projected.reshape(ROWS, GROUP, STEPS, HD).swapaxes(1, 2)
+    projected = projected.astype(BF16).reshape(ROWS, GROUP, STEPS, HD).swapaxes(1, 2)
     return projected.reshape(ROWS, STEPS, WIDTH)
 
 

time: 52.3 us -> 52.2 us (level)
  local copies, waits for them, and re-layouts: 1.65 us -> 0 us
  other arithmetic: 0 us -> 1.62 us
    unnamed x1 -> x0, local copies, waits for them, and re-layouts: 1.65 us -> none
    convert_element_type x0 -> x1, other arithmetic: none -> 1.62 us  [body(): projected.astype(BF16).reshape(ROWS, GROUP, STEPS, HD).swapaxes(1, 2)]
where the time goes in v4:
time: 52.2 us; the launch traced here: 52.1 us
  Pallas kernels  50.4 us (97%)
  other arithmetic  1.62 us (3%)
    pallas_call x1, Pallas kernels, body(): pl.pallas_call(kernel, out_shape=jax.ShapeDtypeStruct((ROWS * SLOT, HD),...  50.4 us
    convert_element_type x1, other arithmetic, body(): projected.astype(BF16).reshape(ROWS, GROUP, STEPS, HD).swapaxes(1, 2)  1.62 us

profile of v4, /device:TPU:1, one launch (start us, length us, event | category | flops | bytes accessed | tf_op | source)
XLA Modules:
  0.0 52.1 jit_solution(1372251578184604779)
XLA Ops:
  0.0 50.4 %shard_map.109 = f32[512,128]{1,0:T(8,128)} custom-call(s32[32]{0:T(128)} %prompt_s.1, s32[32]{0:T(128)} %partner_s.1, s32[32]{0:T(128)} %length_s.1, bf16[32,16,128]{2,1,0:T(8,128)(2,1)} %bitcast.16, bf16[64,128]{1,0:T(8,128)(2,1)} %bitcast.17, bf16[64,128]{1,0:T(8,128)(2,1)} %bitcast.18, bf16[32,256,128]{2,1,0:T(8,128)(2,1)} %ks_hbm.1, ...), custom_call_target="tpu_custom_call" | custom-call | tf_op jit(solution)/shard_map/pallas_call | solution.py:424
  50.5 1.6 %convert_element_type.3 = bf16[512,128]{1,0:T(8,128)(2,1)} convert(f32[512,128]{1,0:T(8,128)} %shard_map.109) | non-fusion elementwise | flops 65536 | bytes 393216 | tf_op jit(solution)/shard_map/convert_element_type | solution.py:458
